TPU v7x, 32 devices: a whole 2x2x4 slice. The times are simulated.
32 devices in a mesh: seq: 8 (over y, x, core), head: 4 (over z).
Axes of the slice: x: 2, y: 2, z: 4, core: 2. Of those that a mesh axis runs over, the one named last changes fastest.
Arguments:
- queries: bfloat16 [8192, 32, 128], P('seq', 'head'), may hold values from -6 to 6
- keys: bfloat16 [8192, 32, 128], P('seq', 'head'), may hold values from -6 to 6
- values: bfloat16 [8192, 32, 128], P('seq', 'head'), may hold values from -6 to 6
- out_grad: bfloat16 [8192, 32, 128], P('seq', 'head'), may hold values from -6 to 6
- level_codes: int32 [21, 8192], P(None, ('seq', 'head')), may hold values from 1 to 16
Outputs:
- query_grad: bfloat16 [8192, 32, 128], P('seq', 'head')
- key_grad: bfloat16 [8192, 32, 128], P('seq', 'head')
- value_grad: bfloat16 [8192, 32, 128], P('seq', 'head')
Inputs may be any that keep to these rules, and one draw needn't show every extreme that they name: `level_codes`: level codes are whole numbers.
All inputs are finite; a program needn't handle non-finite values.
Results may differ from a plain program's by a relative error of at most 0.0052.
Values sent between devices are 32-bit elements; how exact they have to be, the bound alone decides.
No kernel may reach another device: no remote copies, remote signals or barrier semaphores. Data moves between devices by JAX's collectives and lax.ppermute only.
A program may use at most 128 MiB of HBM per device.

v0:
```python
import functools

import jax
import jax.numpy as jnp
from jax import lax
from jax.experimental import pallas as pl
from jax.experimental.pallas import tpu as pltpu
from jax.sharding import PartitionSpec as P

F32 = jnp.float32
BF16 = jnp.bfloat16
MIB = 1 << 20


def bits_of(size):
    return size.bit_length() - 1


def dot(a, b):
    return jnp.dot(a, b, preferred_element_type=F32)


def dot_nt(a, b):
    return lax.dot_general(a, b, (((1,), (1,)), ((), ())), preferred_element_type=F32)


def scaled(row, x):
    return (row * x.astype(F32)).astype(BF16)


def stack_levels(parts, axis):
    return parts[0] if len(parts) == 1 else jnp.concatenate(parts, axis=axis)


def level_sources(chunks):
    found = []
    for j in range(bits_of(chunks)):
        for first in range(0, chunks, 2 << j):
            found.append(range(first, first + (1 << j)))
    return found


def states_kernel(
    k_ref, v_ref, q_far, g_far, kh_ref, vh_ref, level_ref, total_ref, q_near, g_near,
    chunk_ref, sems,
):
    heads = k_ref.shape[1]
    chunks = chunk_ref.shape[0]
    step = pl.program_id(0)

    def fetches(i):
        return [
            pltpu.make_async_copy(q_far.at[i], q_near.at[i], sems.at[0, i]),
            pltpu.make_async_copy(g_far.at[i], g_near.at[i], sems.at[1, i]),
        ]

    for fetch in fetches(step):
        fetch.start()
    kh_ref[0] = jnp.swapaxes(k_ref[...], 0, 1)
    vh_ref[0] = jnp.swapaxes(v_ref[...], 0, 1)
    for h in range(heads):
        chunk_ref[step, h] = dot(kh_ref[0, h].T, vh_ref[0, h])

    @pl.when(step == chunks - 1)
    def _():
        for h in range(heads):
            tiles = [chunk_ref[i, h] for i in range(chunks)]
            total_ref[h] = functools.reduce(jnp.add, tiles)
            for n, sources in enumerate(level_sources(chunks)):
                state = functools.reduce(jnp.add, [tiles[i] for i in sources])
                level_ref[n, h] = state.astype(BF16)
        for i in range(chunks):
            for fetch in fetches(i):
                fetch.wait()


def grads_kernel(
    first_row, core_ref, lam_ref, q_ref, g_ref, state_ref,
    qh_ref, gh_ref, send_ref, keep_ref, grad_ref,
):
    heads, width = q_ref.shape[2:]
    half = heads // 2
    levels = grad_ref.shape[0]
    qh_ref[0] = jnp.swapaxes(q_ref[0], 0, 1)
    gh_ref[0] = jnp.swapaxes(g_ref[0], 0, 1)
    first = pl.program_id(0) == 0
    rows = [lam_ref[first_row + b : first_row + b + 1, :] for b in range(levels)]
    for h in range(heads):
        query_t = qh_ref[0, h].T
        weighted = stack_levels([scaled(row, query_t) for row in rows], 0)
        grad = dot(weighted, gh_ref[0, h])
        for b in range(levels):
            part = grad[b * width : (b + 1) * width]
            grad_ref[b, h] = jnp.where(first, part, grad_ref[b, h] + part)

    for core in range(2):

        @pl.when((pl.program_id(0) == pl.num_programs(0) - 1) & (core_ref[0] == core))
        def _():
            for h in range(heads):
                send_ref[h] = state_ref[h] if core == 0 else grad_ref[0, h]
            for level in range(levels):
                for i in range(half):
                    spot = level * half + i
                    source = state_ref if level == 0 else grad_ref.at[level]
                    keep_ref[spot] = source[core * half + i]
                    send_ref[heads + spot] = source[(1 - core) * half + i]


def make_mask(lam_ref, span, mask_ref):
    tile = mask_ref.shape[0]
    part = min(128, tile)
    source = lax.broadcasted_iota(jnp.int32, (part, part), 0)
    target = lax.broadcasted_iota(jnp.int32, (part, part), 1)
    differ = jnp.where(source <= target, jnp.bitwise_xor(source, target), -1)
    for to in range(0, tile, part):
        lanes = slice(span.start + to, span.start + to + part)
        mask = jnp.where(differ >= 0, lam_ref[0:1, lanes], 0.0)
        for power in range(bits_of(part)):
            mask = jnp.where(differ >= 1 << power, lam_ref[power + 1 : power + 2, lanes], mask)
        mask_ref[to : to + part, to : to + part] = mask
        for at in range(0, tile, part):
            if at < to:
                level = bits_of(at ^ to) + 1
                row = lam_ref[level : level + 1, lanes]
                mask_ref[at : at + part, to : to + part] = jnp.broadcast_to(row, (part, part))
            elif at > to:
                mask_ref[at : at + part, to : to + part] = jnp.zeros((part, part), F32)


def diagonal_tile(key, value, query, grad, mask):
    weight_q = (mask * dot_nt(value, grad)).astype(BF16)
    weight_v = (mask * dot_nt(key, query)).astype(BF16)
    dk = dot(weight_q, query).astype(BF16)
    dv = dot(weight_v, grad).astype(BF16)
    return dot(key.T, weight_q), dk, dv


def first_tile_kernel(
    lam_ref, k_ref, v_ref, q_ref, g_ref, dqt_ref, dq_ref, dk_ref, dv_ref, mask_ref
):
    del dq_ref
    make_mask(lam_ref, slice(0, mask_ref.shape[0]), mask_ref)

    @pl.loop(0, k_ref.shape[1], unroll=4)
    def _(h):
        dqt_ref[h], dk_ref[0, h], dv_ref[0, h] = diagonal_tile(
            k_ref[0, h], v_ref[0, h], q_ref[0, h], g_ref[0, h], mask_ref[...]
        )


def local_kernel(
    flag_ref, lam_ref, k_ref, v_ref, q_ref, g_ref, level_ref, found_ref, dqt_ref, dq_in, dk_in, dv_in,
    dq_ref, dk_ref, dv_ref, gin_ref, mask_ref, half_ref,
):
    del dq_in, dk_in, dv_in
    chunks, heads, tile, width = k_ref.shape
    tile_bits = bits_of(tile)
    first_row = tile_bits + bits_of(chunks) + 1
    groups = level_sources(chunks)
    off = (1 - flag_ref[0]).astype(F32)

    @pl.loop(0, heads, unroll=4)
    def _(h):
        found = found_ref[h]
        half_ref[h] = found.astype(BF16)
        for i in range(chunks):
            gin_ref[i, h] = off * found
        row = lam_ref[first_row : first_row + 1, :tile]
        dqt = dqt_ref[h] + row * dot_nt(half_ref[h], g_ref[0, h])
        dq_ref[0, h] = dqt.astype(BF16).T

    for c in range(1, chunks):
        span = slice(c * tile, (c + 1) * tile)
        make_mask(lam_ref, span, mask_ref)

        @pl.loop(0, heads, unroll=4)
        def _(h):
            query, grad = q_ref[c, h], g_ref[c, h]
            dqt, dk_ref[c, h], dv_ref[c, h] = diagonal_tile(
                k_ref[c, h], v_ref[c, h], query, grad, mask_ref[...]
            )
            dqt = dqt + lam_ref[first_row : first_row + 1, span] * dot_nt(half_ref[h], grad)
            query_t = query.T
            for j in range(bits_of(chunks)):
                if c >> j & 1:
                    row = lam_ref[tile_bits + 1 + j : tile_bits + 2 + j, span]
                    first = (c >> j ^ 1) << j
                    sources = range(first, first + (1 << j))
                    dqt = dqt + row * dot_nt(level_ref[groups.index(sources), h], grad)
                    part = dot(scaled(row, query_t), grad)
                    for i in sources:
                        gin_ref[i, h] = gin_ref[i, h] + part
            dq_ref[c, h] = dqt.astype(BF16).T


def pair_kernel(flag_ref, keep_ref, found_ref, *out_refs):
    half = out_refs[0].shape[0]
    heads = found_ref.shape[0] - keep_ref.shape[0]

    def pair(level, i):
        return keep_ref[level * half + i] + found_ref[heads + level * half + i]

    for n, out_ref in enumerate(out_refs):
        for on in range(2):

            @pl.when(flag_ref[n + 1] == on)
            def _():
                for i in range(half):
                    out_ref[i] = pair((n + 1) * on, i)


def sum_kernel(counts, *refs):
    out_ref = refs[-1]
    at = 0
    for n, count in enumerate(counts):
        for i in range(out_ref.shape[1]):
            out_ref[n, i] = functools.reduce(jnp.add, [r[i] for r in refs[at : at + count]])
        at += count


def widen(lam_ref, first_row, lanes, wide_ref):
    for b in range(wide_ref.shape[0]):
        row = lam_ref[first_row + b : first_row + b + 1, lanes]
        wide_ref[b] = jnp.broadcast_to(row, wide_ref.shape[:0:-1]).T


def received(flag_ref, sums_ref, i):
    parts = [sums_ref[b, i] for b in range(sums_ref.shape[0])]
    off = [(1 - flag_ref[b + 1]).astype(F32) for b in range(len(parts))]
    state = functools.reduce(jnp.add, [w * part for w, part in zip(off, parts)])
    return stack_levels([part.astype(BF16) for part in parts], 0), state


def add_received(half, state, wide_ref, key, value, grad, dq, dk, dv):
    width = key.shape[1]
    dq = dq.astype(F32)
    projected = dot_nt(grad, half)
    for b in range(wide_ref.shape[0]):
        dq = dq + wide_ref[b] * projected[:, b * width : (b + 1) * width]
    state = state.astype(BF16)
    none = jnp.zeros((width, width), BF16)
    right = jnp.concatenate(
        [
            jnp.concatenate([state.T, none], axis=1),
            jnp.concatenate([none, state], axis=1),
        ],
        axis=0,
    )
    product = dot(jnp.concatenate([value, key], axis=1), right)
    dk = dk.astype(F32) + product[:, :width]
    dv = dv.astype(F32) + product[:, width:]
    return dq.astype(BF16), dk.astype(BF16), dv.astype(BF16)


def own_half_kernel(
    first_row, flag_ref, lam_ref, k_ref, v_ref, g_ref, gin_ref, sums_ref, dq_in, dk_in, dv_in,
    dq_ref, dk_ref, dv_ref, wide_ref, half_ref, state_ref,
):
    chunks, _, tile, _ = k_ref.shape
    half = half_ref.shape[0]
    start = flag_ref[0] * half
    for i in range(half):
        half_ref[i], state_ref[i] = received(flag_ref, sums_ref, i)
    for c in range(chunks):
        widen(lam_ref, first_row, slice(c * tile, (c + 1) * tile), wide_ref)
        for i in range(half):
            h = start + i
            dq_ref[c, h], dk_ref[c, h], dv_ref[c, h] = add_received(
                half_ref[i], gin_ref[c, h] + state_ref[i], wide_ref,
                k_ref[c, h], v_ref[c, h], g_ref[c, h],
                dq_in[c, h], dk_in[c, h], dv_in[c, h],
            )


def final_kernel(
    first_row, flag_ref, lam_ref, k_ref, v_ref, g_ref, dq_in, dk_in, dv_in, gin_ref, sums_ref,
    dq_ref, dk_ref, dv_ref, wide_ref, half_ref, state_ref,
):
    heads = k_ref.shape[1]
    half = half_ref.shape[0]

    @pl.when(pl.program_id(0) == 0)
    def _():
        for i in range(half):
            half_ref[i], state_ref[i] = received(flag_ref, sums_ref, i)

    widen(lam_ref, first_row, slice(None), wide_ref)
    for core in range(2):

        @pl.when(flag_ref[0] == core)
        def _():
            done = []
            for h in range(heads):
                parts = [x[0, h] for x in (dq_in, dk_in, dv_in)]
                if h // half != core:
                    i = h % half
                    parts = add_received(
                        half_ref[i], gin_ref[0, h] + state_ref[i], wide_ref,
                        k_ref[0, h], v_ref[0, h], g_ref[0, h], *parts,
                    )
                done.append(parts)
            for out_ref, parts in zip((dq_ref, dk_ref, dv_ref), zip(*done)):
                out_ref[...] = jnp.swapaxes(jnp.stack(parts), 0, 1)


def shape(dims, dtype):
    return jax.ShapeDtypeStruct(dims, dtype)


def params(limit):
    return pltpu.CompilerParams(vmem_limit_bytes=limit * MIB)


def cost(flops, size):
    return pl.CostEstimate(flops=int(flops), bytes_accessed=int(size), transcendentals=0)


def on_device(queries, keys, values, out_grad, level_codes):
    count, heads, width = queries.shape
    scale = width ** (-0.5)
    local_bits = bits_of(count)
    blocks = lax.axis_size("seq")
    tree_bits = bits_of(blocks)
    groups = lax.axis_size("head")
    here = lax.axis_index("seq")
    tile = min(256, count)
    chunks = count // tile
    half = heads // 2
    rows = local_bits + 1 + tree_bits
    flags = jnp.bitwise_and(jnp.right_shift(here, jnp.arange(max(tree_bits, 1))), 1)

    def permute(x, apart):
        return lax.ppermute(x, "seq", [(i, i ^ apart) for i in range(blocks)])

    def in_hbm(*arrays):
        return [pltpu.with_memory_space_constraint(x, pltpu.HBM) for x in arrays]

    def near(*arrays):
        return [pltpu.with_memory_space_constraint(x, pltpu.VMEM) for x in arrays]

    token_block = pl.BlockSpec((tile, heads, width), lambda c: (c, 0, 0))
    lam_block = pl.BlockSpec((rows, tile), lambda c: (0, c))
    in_smem = pl.BlockSpec(memory_space=pltpu.SMEM)
    in_vmem = pl.BlockSpec(memory_space=pltpu.VMEM)
    anywhere = pl.BlockSpec(memory_space=pl.ANY)

    def chunk_block(*dims):
        return pl.BlockSpec((1,) + dims, lambda c: (c,) + (0,) * len(dims))

    def whole(*dims):
        return pl.BlockSpec(dims, lambda c: (0,) * len(dims))

    head_block = chunk_block(heads, tile, width)
    natural = pltpu.VMEM((chunks, heads, tile, width), BF16)
    square = (width, width)
    size = count * heads * width
    groups_in = len(level_sources(chunks))
    queries, out_grad = [x.reshape(chunks, tile, heads, width) for x in (queries, out_grad)]
    queries, keys, values, out_grad = in_hbm(queries, keys, values, out_grad)

    kh, vh, level_state, state, queries, out_grad = pl.pallas_call(
        states_kernel,
        grid=(chunks,),
        in_specs=[token_block, token_block, anywhere, anywhere],
        out_specs=[
            head_block, head_block, whole(groups_in, heads, *square), whole(heads, *square),
            in_vmem, in_vmem,
        ],
        out_shape=[
            natural, natural, pltpu.VMEM((groups_in, heads, *square), BF16),
            pltpu.VMEM((heads, *square), F32),
            *[pltpu.VMEM((chunks, tile, heads, width), BF16)] * 2,
        ],
        scratch_shapes=[
            pltpu.VMEM((chunks, heads, *square), F32),
            pltpu.SemaphoreType.DMA((2, chunks)),
        ],
        compiler_params=params(10),
        cost_estimate=cost(2 * size * width, 8 * size),
        name="states",
    )(keys, values, queries, out_grad)

    group = lax.axis_index("head")
    pieces = [
        lax.ppermute(level_codes, "head", [(i, (i + r) % groups) for i in range(groups)])
        for r in range(1, groups)
    ]
    pieces, state = lax.optimization_barrier((pieces, state))
    pieces = jnp.stack([level_codes, *pieces])
    codes = jnp.concatenate(
        [
            lax.dynamic_index_in_dim(pieces, (group - j) % groups, 0, keepdims=False)[:rows]
            for j in range(groups)
        ],
        axis=1,
    )
    order = jnp.arange(rows)
    factor = jnp.exp2(-0.5 * jnp.maximum(order.astype(F32) - 1.0, 0.0)) / 16.0
    on_bit = jnp.bitwise_and(jnp.right_shift(here, jnp.maximum(order - local_bits - 1, 0)), 1)
    factor = jnp.where(order > local_bits, factor * on_bit.astype(F32), factor)
    lam = codes.astype(F32) * (scale * factor)[:, None]

    qh, gh, send, keep = pl.pallas_call(
        functools.partial(grads_kernel, local_bits + 1),
        grid=(chunks,),
        in_specs=[in_smem, lam_block, *[chunk_block(tile, heads, width)] * 2, whole(heads, *square)],
        out_specs=[
            head_block, head_block,
            whole(heads + tree_bits * half, *square), whole(tree_bits * half, *square),
        ],
        out_shape=[
            natural, natural,
            pltpu.VMEM((heads + tree_bits * half, *square), F32),
            pltpu.VMEM((tree_bits * half, *square), F32),
        ],
        scratch_shapes=[pltpu.VMEM((tree_bits, heads, *square), F32)],
        compiler_params=params(10),
        cost_estimate=cost(2 * tree_bits * size * width, 8 * size),
        name="level_grads",
    )(flags, lam, *near(queries, out_grad, state))
    found = permute(send, 1)
    kh, vh, qh, gh, level_state, keep = near(kh, vh, qh, gh, level_state, keep)

    dqt, *parts = pl.pallas_call(
        first_tile_kernel,
        in_specs=[in_vmem] * 5,
        out_specs=[in_vmem] * 4,
        out_shape=[pltpu.VMEM((heads, width, tile), F32)] + [natural] * 3,
        scratch_shapes=[pltpu.VMEM((tile, tile), F32)],
        compiler_params=params(6),
        cost_estimate=cost(14 * size * tile / chunks, 4 * size),
        name="first_tile",
    )(lam, kh, vh, qh, gh)
    messages = pl.pallas_call(
        pair_kernel,
        in_specs=[in_smem, in_vmem, in_vmem],
        out_specs=[in_vmem] * (tree_bits - 1),
        out_shape=[pltpu.VMEM((half, *square), F32)] * (tree_bits - 1),
        compiler_params=params(4),
        cost_estimate=cost(size, size),
        name="pair",
    )(flags, keep, found)
    *messages, parts = lax.optimization_barrier((*messages, parts))
    arrived = [
        [permute(messages[b - 1], 1 << b | m) for m in range(0, 1 << b, 2)]
        for b in range(1, tree_bits)
    ]
    *parts, gin = pl.pallas_call(
        local_kernel,
        in_specs=[in_smem] + [in_vmem] * 8 + [anywhere] * 3,
        out_specs=[in_vmem] * 4,
        out_shape=[natural] * 3 + [pltpu.VMEM((chunks, heads, *square), F32)],
        input_output_aliases={9: 0, 10: 1, 11: 2},
        scratch_shapes=[pltpu.VMEM((tile, tile), F32), pltpu.VMEM((heads, *square), BF16)],
        compiler_params=params(6),
        cost_estimate=cost(14 * size * tile, 4 * size),
        name="local",
    )(flags, lam, kh, vh, qh, gh, level_state, found, *near(dqt, *parts))
    arrived, parts = lax.optimization_barrier((arrived, parts))
    flat = [x for some in arrived for x in some]
    sums_shape = (tree_bits - 1, half, *square)
    mine = pl.pallas_call(
        functools.partial(sum_kernel, [len(some) for some in arrived]),
        in_specs=[in_vmem] * len(flat),
        out_specs=in_vmem,
        out_shape=pltpu.VMEM(sums_shape, F32),
        compiler_params=params(6),
        cost_estimate=cost(size, size),
        name="sums",
    )(*flat)
    others = permute(mine, 1)

    kept = [
        pltpu.VMEM((tree_bits - 1, tile, width), F32),
        pltpu.VMEM((half, (tree_bits - 1) * width, width), BF16),
        pltpu.VMEM((half, *square), F32),
    ]
    gin, mine = near(gin, mine)
    parts = pl.pallas_call(
        functools.partial(own_half_kernel, local_bits + 2),
        in_specs=[in_smem] + [in_vmem] * 9,
        out_specs=[in_vmem] * 3,
        out_shape=[natural] * 3,
        input_output_aliases={7: 0, 8: 1, 9: 2},
        scratch_shapes=kept,
        compiler_params=params(6),
        cost_estimate=cost((tree_bits + 2) * size * width, 8 * size),
        name="own_half",
    )(flags, lam, kh, vh, gh, gin, mine, *near(*parts))
    others, parts = lax.optimization_barrier((others, parts))
    return pl.pallas_call(
        functools.partial(final_kernel, local_bits + 2),
        grid=(chunks,),
        in_specs=[
            in_smem, lam_block, *[head_block] * 6, chunk_block(heads, *square), whole(*sums_shape),
        ],
        out_specs=[token_block] * 3,
        out_shape=[shape((count, heads, width), BF16)] * 3,
        scratch_shapes=kept,
        compiler_params=params(12),
        cost_estimate=cost((tree_bits + 2) * size * width, 16 * size),
        name="final",
    )(flags, lam, kh, vh, gh, *near(*parts), gin, others)


def solution(mesh):
    tokens = P("seq", "head", None)
    return jax.shard_map(
        on_device,
        mesh=mesh,
        in_specs=(tokens, tokens, tokens, tokens, P(None, ("seq", "head"))),
        out_specs=(tokens, tokens, tokens),
        check_vma=False,
    )
```

profile of v0, /device:TPU:0, one launch (start us, length us, event | category | flops | bytes accessed | tf_op | source)
XLA Modules:
  0.0 44.5 jit_solution(9902923352492527064)
XLA Ops:
  0.6 3.1 %collective-permute-start = (s32[21,256]{1,0:T(8,128)}, s32[21,256]{1,0:T(8,128)S(1)}, u32[]{:S(2)}, u32[]{:S(2)}) collective-permute-start(s32[21,256]{1,0:T(8,128)} %param.9), channel_id=1, source_target_pairs={{0,1},{1,2},{2,3},{3,0},{4,5},{5,6},{6,7},{7,4},{8,9},{9,10},{10,1... | collective-permute-start | bytes 64520 | tf_op jit(solution)/shard_map/ppermute | solution.py:386
  3.7 2.6 %collective-permute-start.1 = (s32[21,256]{1,0:T(8,128)}, s32[21,256]{1,0:T(8,128)S(1)}, u32[]{:S(2)}, u32[]{:S(2)}) collective-permute-start(s32[21,256]{1,0:T(8,128)} %param.9), channel_id=1, source_target_pairs={{0,2},{1,3},{2,0},{3,1},{4,6},{5,7},{6,4},{7,5},{8,10},{9,11},{10,... | collective-permute-start | bytes 64520 | tf_op jit(solution)/shard_map/ppermute | solution.py:386
  6.3 1.3 %collective-permute-start.2 = (s32[21,256]{1,0:T(8,128)}, s32[21,256]{1,0:T(8,128)S(1)}, u32[]{:S(2)}, u32[]{:S(2)}) collective-permute-start(s32[21,256]{1,0:T(8,128)} %param.9), channel_id=1, source_target_pairs={{0,3},{1,0},{2,1},{3,2},{4,7},{5,4},{6,5},{7,6},{8,11},{9,8},{10,9... | collective-permute-start | bytes 64520 | tf_op jit(solution)/shard_map/ppermute | solution.py:386
  7.7 0.0 copy-start
  7.7 5.4 %states.1 = (bf16[4,8,256,128]{3,2,1,0:T(8,128)(2,1)S(1)}, bf16[4,8,256,128]{3,2,1,0:T(8,128)(2,1)S(1)}, bf16[3,8,128,128]{3,2,1,0:T(8,128)(2,1)S(1)}, f32[8,128...) custom-call(bf16[1024,8,128]{2,1,0:T(8,128)(2,1)} %k_ref.1, ...), custom_call_target="tpu_custom_call" | custom-call | flops 268435456 | bytes 8388608 | tf_op jit(solution)/shard_map/states/pallas_call | solution.py:362
  13.1 0.0 collective-permute-done
  13.2 0.0 collective-permute-done.1
  13.2 0.0 collective-permute-done.2
  13.2 0.0 copy-done
  13.2 0.1 fusion.lam_ref
  13.3 4.8 %level_grads.1 = (bf16[4,8,256,128]{3,2,1,0:T(8,128)(2,1)S(1)}, bf16[4,8,256,128]{3,2,1,0:T(8,128)(2,1)S(1)}, f32[20,128,128]{2,1,0:T(8,128)S(1)}, f32[12,128,128]{2,1,0:T(8,128)S(1)}) custom-call(s32[3]{0:T(128)S(1)} %shift-right-arithmetic_and_fusion.core_ref.flag_ref, f32[14,1024]{1,0:T(8,128)S(1)} %fusion.lam_ref, ...), custom_call_target="tpu_custom_call" | custom-call | flops 805306368 | bytes 8388608 | tf_op jit(solution)/shard_map/level_grads/pallas_call | solution.py:404
  18.1 0.1 collective-permute-start.3
  18.2 2.2 %first_tile.1 = (f32[8,128,256]{2,1,0:T(8,128)S(1)}, bf16[4,8,256,128]{3,2,1,0:T(8,128)(2,1)S(1)}, bf16[4,8,256,128]{3,2,1,0:T(8,128)(2,1)S(1)}, bf16[4,8,256,128]{3,2,1,0:T(8,128)(2,1)S(1)}) custom-call(f32[14,1024]{1,0:T(8,128)S(1)} %fusion.lam_ref, bf16[4,8,256,128]{3,2,1,0:T(8,128)(2,1)S(1)} %get-tuple-element.49.k_ref, ...), custom_call_target="tpu_custom_call" | custom-call | flops 939524096 | bytes 4194304 | tf_op jit(solution)/shard_map/first_tile/pallas_call | solution.py:425
  20.4 0.9 %collective-permute-done.3.found_ref = f32[20,128,128]{2,1,0:T(8,128)S(1)} collective-permute-done((f32[20,128,128]{2,1,0:T(8,128)S(1)}, f32[20,128,128]{2,1,0:T(8,128)S(1)}, u32[]{:S(2)}, u32[]{:S(2)}) %collective-permute-start.3) | collective-permute-done | bytes 1310752 | tf_op jit(solution)/shard_map/ppermute | solution.py:334
  21.2 0.6 %pair.1 = (f32[4,128,128]{2,1,0:T(8,128)S(1)}, f32[4,128,128]{2,1,0:T(8,128)S(1)}) custom-call(s32[3]{0:T(128)S(1)} %shift-right-arithmetic_and_fusion.core_ref.flag_ref, f32[12,128,128]{2,1,0:T(8,128)S(1)} %get-tuple-element.55.keep_ref, f32[20,128,128]{2,1,0:T(8,128)S(1)} %collective-permute-done.3.found_ref), custom_call_target="tpu_custom_call" | custom-call | flops 1048576 | bytes 1048576 | tf_op jit(solution)/shard_map/pair/pallas_call | solution.py:435
  21.8 1.6 %collective-permute-start.5 = (f32[4,128,128]{2,1,0:T(8,128)S(1)}, f32[4,128,128]{2,1,0:T(8,128)S(1)}, u32[]{:S(2)}, u32[]{:S(2)}) collective-permute-start(f32[4,128,128]{2,1,0:T(8,128)S(1)} %get-tuple-element.64), channel_id=1, source_target_pairs={{0,16},{4,20},{8,24},{12,28},{16,0},{20,4},{24,8},{28,12},{1,17},{... | collective-permute-start | bytes 786440 | tf_op jit(solution)/shard_map/ppermute | solution.py:334
  23.4 1.4 %collective-permute-start.6 = (f32[4,128,128]{2,1,0:T(8,128)S(1)}, f32[4,128,128]{2,1,0:T(8,128)S(1)}, u32[]{:S(2)}, u32[]{:S(2)}) collective-permute-start(f32[4,128,128]{2,1,0:T(8,128)S(1)} %get-tuple-element.64), channel_id=1, source_target_pairs={{0,24},{4,28},{8,16},{12,20},{16,8},{20,12},{24,0},{28,4},{1,25},{... | collective-permute-start | bytes 786440 | tf_op jit(solution)/shard_map/ppermute | solution.py:334
  24.9 0.5 %collective-permute-start.4 = (f32[4,128,128]{2,1,0:T(8,128)S(1)}, f32[4,128,128]{2,1,0:T(8,128)S(1)}, u32[]{:S(2)}, u32[]{:S(2)}) collective-permute-start(f32[4,128,128]{2,1,0:T(8,128)S(1)} %get-tuple-element.63), channel_id=1, source_target_pairs={{0,8},{4,12},{8,0},{12,4},{16,24},{20,28},{24,16},{28,20},{1,9},{5... | collective-permute-start | bytes 786440 | tf_op jit(solution)/shard_map/ppermute | solution.py:334
  25.4 9.7 %local.1 = (bf16[4,8,256,128]{3,2,1,0:T(8,128)(2,1)S(1)}, bf16[4,8,256,128]{3,2,1,0:T(8,128)(2,1)S(1)}, bf16[4,8,256,128]{3,2,1,0:T(8,128)(2,1)S(1)}, f32[4,8,128,128]{3,2,1,0:T(8,128)S(1)}) custom-call(s32[3]{0:T(128)S(1)} %shift-right-arithmetic_and_fusion.core_ref.flag_ref, ...), custom_call_target="tpu_custom_call", output_to_operand_aliasing={{0}: (9, {}), {1}: (10, {}), {2}: (11, {})} | custom-call | flops 3758096384 | bytes 4194304 | tf_op jit(solution)/shard_map/local/pallas_call | solution.py:449
  35.1 2.0 %collective-permute-done.4.refs_0_ = f32[4,128,128]{2,1,0:T(8,128)S(1)} collective-permute-done((f32[4,128,128]{2,1,0:T(8,128)S(1)}, f32[4,128,128]{2,1,0:T(8,128)S(1)}, u32[]{:S(2)}, u32[]{:S(2)}) %collective-permute-start.4) | collective-permute-done | bytes 262176 | tf_op jit(solution)/shard_map/ppermute | solution.py:334
  37.1 0.0 collective-permute-done.5.refs_1_
  37.1 0.0 collective-permute-done.6.refs_2_
  37.2 0.1 collective-permute-start.7
  37.2 2.0 %own_half.1 = (bf16[4,8,256,128]{3,2,1,0:T(8,128)(2,1)S(1)}, bf16[4,8,256,128]{3,2,1,0:T(8,128)(2,1)S(1)}, bf16[4,8,256,128]{3,2,1,0:T(8,128)(2,1)S(1)}) custom-call(s32[3]{0:T(128)S(1)} %shift-right-arithmetic_and_fusion.core_ref.flag_ref, f32[14,1024]{1,0:T(8,128)S(1)} %fusion.lam_ref, ...), custom_call_target="tpu_custom_call", output_to_operand_aliasing={{0}: (7, {}), {1}: (8, {}), {2}: (9, {})} | custom-call | flops 671088640 | bytes 8388608 | tf_op jit(solution)/shard_map/own_half/pallas_call | solution.py:480
  39.2 0.0 collective-permute-done.7.sums_ref
  39.2 5.2 %final.1 = (bf16[1024,8,128]{2,1,0:T(8,128)(2,1)}, bf16[1024,8,128]{2,1,0:T(8,128)(2,1)}, bf16[1024,8,128]{2,1,0:T(8,128)(2,1)}) custom-call(s32[3]{0:T(128)S(1)} %shift-right-arithmetic_and_fusion.core_ref.flag_ref, f32[14,1024]{1,0:T(8,128)S(1)} %fusion.lam_ref, bf16[4,8,256,128]{3,2,1,0:T(8,128)(2,1)S(1)} %get-tuple-element.49.k_ref, ...), custom_call_target="tpu_custom_call" | custom-call | flops 671088640 | bytes 16777216 | tf_op jit(solution)/shard_map/final/pallas_call | solution.py:492
  (5 shorter events, 0.1 us)
Async XLA Ops:
  0.6 12.5 %collective-permute-start = (s32[21,256]{1,0:T(8,128)}, s32[21,256]{1,0:T(8,128)S(1)}, u32[]{:S(2)}, u32[]{:S(2)}) collective-permute-start(s32[21,256]{1,0:T(8,128)} %param.9), channel_id=1, source_target_pairs={{0,1},{1,2},{2,3},{3,0},{4,5},{5,6},{6,7},{7,4},{8,9},{9,10},{10,1... | collective-permute-start | bytes 64520 | tf_op jit(solution)/shard_map/ppermute | solution.py:386
  3.7 9.4 %collective-permute-start.1 = (s32[21,256]{1,0:T(8,128)}, s32[21,256]{1,0:T(8,128)S(1)}, u32[]{:S(2)}, u32[]{:S(2)}) collective-permute-start(s32[21,256]{1,0:T(8,128)} %param.9), channel_id=1, source_target_pairs={{0,2},{1,3},{2,0},{3,1},{4,6},{5,7},{6,4},{7,5},{8,10},{9,11},{10,... | collective-permute-start | bytes 64520 | tf_op jit(solution)/shard_map/ppermute | solution.py:386
  6.3 6.9 %collective-permute-start.2 = (s32[21,256]{1,0:T(8,128)}, s32[21,256]{1,0:T(8,128)S(1)}, u32[]{:S(2)}, u32[]{:S(2)}) collective-permute-start(s32[21,256]{1,0:T(8,128)} %param.9), channel_id=1, source_target_pairs={{0,3},{1,0},{2,1},{3,2},{4,7},{5,4},{6,5},{7,6},{8,11},{9,8},{10,9... | collective-permute-start | bytes 64520 | tf_op jit(solution)/shard_map/ppermute | solution.py:386
  7.7 5.5 %copy-start = (s32[21,256]{1,0:T(8,128)S(1)}, s32[21,256]{1,0:T(8,128)}, u32[]{:S(2)}) copy-start(s32[21,256]{1,0:T(8,128)} %param.9) | copy-start | bytes 64516
  18.1 3.1 %collective-permute-start.3 = (f32[20,128,128]{2,1,0:T(8,128)S(1)}, f32[20,128,128]{2,1,0:T(8,128)S(1)}, u32[]{:S(2)}, u32[]{:S(2)}) collective-permute-start(f32[20,128,128]{2,1,0:T(8,128)S(1)} %get-tuple-element.56), channel_id=1, source_target_pairs={{0,4},{4,0},{8,12},{12,8},{16,20},{20,16},{24,28},{28,24},{1,5},{5... | collective-permute-start | bytes 3932168 | tf_op jit(solution)/shard_map/ppermute | solution.py:334
  21.8 15.3 %collective-permute-start.5 = (f32[4,128,128]{2,1,0:T(8,128)S(1)}, f32[4,128,128]{2,1,0:T(8,128)S(1)}, u32[]{:S(2)}, u32[]{:S(2)}) collective-permute-start(f32[4,128,128]{2,1,0:T(8,128)S(1)} %get-tuple-element.64), channel_id=1, source_target_pairs={{0,16},{4,20},{8,24},{12,28},{16,0},{20,4},{24,8},{28,12},{1,17},{... | collective-permute-start | bytes 786440 | tf_op jit(solution)/shard_map/ppermute | solution.py:334
  23.4 13.7 %collective-permute-start.6 = (f32[4,128,128]{2,1,0:T(8,128)S(1)}, f32[4,128,128]{2,1,0:T(8,128)S(1)}, u32[]{:S(2)}, u32[]{:S(2)}) collective-permute-start(f32[4,128,128]{2,1,0:T(8,128)S(1)} %get-tuple-element.64), channel_id=1, source_target_pairs={{0,24},{4,28},{8,16},{12,20},{16,8},{20,12},{24,0},{28,4},{1,25},{... | collective-permute-start | bytes 786440 | tf_op jit(solution)/shard_map/ppermute | solution.py:334
  24.9 12.2 %collective-permute-start.4 = (f32[4,128,128]{2,1,0:T(8,128)S(1)}, f32[4,128,128]{2,1,0:T(8,128)S(1)}, u32[]{:S(2)}, u32[]{:S(2)}) collective-permute-start(f32[4,128,128]{2,1,0:T(8,128)S(1)} %get-tuple-element.63), channel_id=1, source_target_pairs={{0,8},{4,12},{8,0},{12,4},{16,24},{20,28},{24,16},{28,20},{1,9},{5... | collective-permute-start | bytes 786440 | tf_op jit(solution)/shard_map/ppermute | solution.py:334
  37.2 2.1 %collective-permute-start.7 = (f32[2,4,128,128]{3,2,1,0:T(8,128)S(1)}, f32[2,4,128,128]{3,2,1,0:T(8,128)S(1)}, u32[]{:S(2)}, u32[]{:S(2)}) collective-permute-start(f32[2,4,128,128]{3,2,1,0:T(8,128)S(1)} %sums.1.sums_ref), channel_id=1, source_target_pairs={{0,4},{4,0},{8,12},{12,8},{16,20},{20,16},{24,28},{28,24},{1,5},{5... | collective-permute-start | bytes 1572872 | tf_op jit(solution)/shard_map/ppermute | solution.py:334
where the time goes:
time: 44.8 us; the launch traced here: 44.5 us
  Pallas kernels  30 us (67%)
  starting transfers between devices  10.7 us (24%)
  waiting for transfers between devices  2.86 us (6%)
  between operations  0.79 us (2%)
    pallas_call x1, Pallas kernels, on_device(): pl.pallas_call(local_kernel, in_specs=[in_smem] + [in_vmem] * 8 + [anywhe...  9.7 us
    ppermute x3, starting transfers between devices, on_device(): lax.ppermute(level_codes, 'head', [(i, (i + r) % groups) for i in range(g...  7.01 us
    pallas_call x1, Pallas kernels, on_device(): pl.pallas_call(states_kernel, grid=(chunks,), in_specs=[token_block, toke...  5.43 us
    pallas_call x1, Pallas kernels, on_device(): pl.pallas_call(functools.partial(final_kernel, local_bits + 2), grid=(chu...  5.21 us
    pallas_call x1, Pallas kernels, on_device(): pl.pallas_call(functools.partial(grads_kernel, local_bits + 1), grid=(chu...  4.81 us
    ppermute x5, starting transfers between devices, permute(): return lax.ppermute(x, 'seq', [(i, i ^ apart) for i in range(blocks)])  3.7 us
    ppermute x5, waiting for transfers between devices, permute(): return lax.ppermute(x, 'seq', [(i, i ^ apart) for i in range(blocks)])  2.85 us
    pallas_call x1, Pallas kernels, on_device(): pl.pallas_call(first_tile_kernel, in_specs=[in_vmem] * 5, out_specs=[in_v...  2.16 us
  transfers between devices with their start and end apart: 8, of which 2 were waited for; matrix products, arithmetic and copies ran while one was open for 0% of the time, Pallas kernels for 43%

commit v1 on v0

--- a/solution.py
+++ b/solution.py
@@ -40,22 +40,10 @@
     return found
 
 
-def states_kernel(
-    k_ref, v_ref, q_far, g_far, kh_ref, vh_ref, level_ref, total_ref, q_near, g_near,
-    chunk_ref, sems,
-):
+def states_kernel(k_ref, v_ref, kh_ref, vh_ref, level_ref, total_ref, chunk_ref):
     heads = k_ref.shape[1]
     chunks = chunk_ref.shape[0]
     step = pl.program_id(0)
-
-    def fetches(i):
-        return [
-            pltpu.make_async_copy(q_far.at[i], q_near.at[i], sems.at[0, i]),
-            pltpu.make_async_copy(g_far.at[i], g_near.at[i], sems.at[1, i]),
-        ]
-
-    for fetch in fetches(step):
-        fetch.start()
     kh_ref[0] = jnp.swapaxes(k_ref[...], 0, 1)
     vh_ref[0] = jnp.swapaxes(v_ref[...], 0, 1)
     for h in range(heads):
@@ -69,25 +57,24 @@
             for n, sources in enumerate(level_sources(chunks)):
                 state = functools.reduce(jnp.add, [tiles[i] for i in sources])
                 level_ref[n, h] = state.astype(BF16)
-        for i in range(chunks):
-            for fetch in fetches(i):
-                fetch.wait()
 
 
 def grads_kernel(
-    first_row, core_ref, lam_ref, q_ref, g_ref, state_ref,
+    flag_ref, factor_ref, codes_ref, q_ref, g_ref, state_ref,
     qh_ref, gh_ref, send_ref, keep_ref, grad_ref,
 ):
-    heads, width = q_ref.shape[2:]
+    heads, width = q_ref.shape[1:]
     half = heads // 2
-    levels = grad_ref.shape[0]
-    qh_ref[0] = jnp.swapaxes(q_ref[0], 0, 1)
-    gh_ref[0] = jnp.swapaxes(g_ref[0], 0, 1)
+    levels, tile = codes_ref.shape
+    qh_ref[0] = jnp.swapaxes(q_ref[...], 0, 1)
+    gh_ref[0] = jnp.swapaxes(g_ref[...], 0, 1)
     first = pl.program_id(0) == 0
-    rows = [lam_ref[first_row + b : first_row + b + 1, :] for b in range(levels)]
+    rows = [
+        jnp.broadcast_to(codes_ref[b : b + 1, :], (width, tile)).astype(BF16) for b in range(levels)
+    ]
     for h in range(heads):
         query_t = qh_ref[0, h].T
-        weighted = stack_levels([scaled(row, query_t) for row in rows], 0)
+        weighted = stack_levels([row * query_t for row in rows], 0)
         grad = dot(weighted, gh_ref[0, h])
         for b in range(levels):
             part = grad[b * width : (b + 1) * width]
@@ -95,16 +82,20 @@
 
     for core in range(2):
 
-        @pl.when((pl.program_id(0) == pl.num_programs(0) - 1) & (core_ref[0] == core))
+        @pl.when((pl.program_id(0) == pl.num_programs(0) - 1) & (flag_ref[0] == core))
         def _():
             for h in range(heads):
-                send_ref[h] = state_ref[h] if core == 0 else grad_ref[0, h]
+                send_ref[h] = state_ref[h] if core == 0 else factor_ref[0] * grad_ref[0, h]
             for level in range(levels):
                 for i in range(half):
                     spot = level * half + i
-                    source = state_ref if level == 0 else grad_ref.at[level]
-                    keep_ref[spot] = source[core * half + i]
-                    send_ref[heads + spot] = source[(1 - core) * half + i]
+                    mine, other = core * half + i, (1 - core) * half + i
+                    if level == 0:
+                        keep_ref[spot] = state_ref[mine]
+                        send_ref[heads + spot] = state_ref[other]
+                    else:
+                        keep_ref[spot] = factor_ref[level] * grad_ref[level, mine]
+                        send_ref[heads + spot] = factor_ref[level] * grad_ref[level, other]
 
 
 def make_mask(lam_ref, span, mask_ref):
@@ -194,29 +185,28 @@
             dq_ref[c, h] = dqt.astype(BF16).T
 
 
-def pair_kernel(flag_ref, keep_ref, found_ref, *out_refs):
+def pair_kernel(levels, flag_ref, keep_ref, found_ref, *out_refs):
     half = out_refs[0].shape[0]
     heads = found_ref.shape[0] - keep_ref.shape[0]
 
     def pair(level, i):
         return keep_ref[level * half + i] + found_ref[heads + level * half + i]
 
-    for n, out_ref in enumerate(out_refs):
+    for b, out_ref in zip(levels, out_refs):
         for on in range(2):
 
-            @pl.when(flag_ref[n + 1] == on)
+            @pl.when(flag_ref[b] == on)
             def _():
                 for i in range(half):
-                    out_ref[i] = pair((n + 1) * on, i)
-
-
-def sum_kernel(counts, *refs):
+                    out_ref[i] = pair(b * on, i)
+
+
+def sum_kernel(levels, *refs):
     out_ref = refs[-1]
-    at = 0
-    for n, count in enumerate(counts):
+    for n in range(out_ref.shape[0]):
         for i in range(out_ref.shape[1]):
-            out_ref[n, i] = functools.reduce(jnp.add, [r[i] for r in refs[at : at + count]])
-        at += count
+            parts = [ref[i] for b, ref in zip(levels, refs) if b == n + 1]
+            out_ref[n, i] = functools.reduce(jnp.add, parts)
 
 
 def widen(lam_ref, first_row, lanes, wide_ref):
@@ -232,12 +222,17 @@
     return stack_levels([part.astype(BF16) for part in parts], 0), state
 
 
-def add_received(half, state, wide_ref, key, value, grad, dq, dk, dv):
-    width = key.shape[1]
+def add_to_query(half, wide_ref, grad, dq):
+    width = grad.shape[1]
     dq = dq.astype(F32)
     projected = dot_nt(grad, half)
     for b in range(wide_ref.shape[0]):
         dq = dq + wide_ref[b] * projected[:, b * width : (b + 1) * width]
+    return dq.astype(BF16)
+
+
+def add_to_key_value(state, key, value, dk, dv):
+    width = key.shape[1]
     state = state.astype(BF16)
     none = jnp.zeros((width, width), BF16)
     right = jnp.concatenate(
@@ -250,7 +245,7 @@
     product = dot(jnp.concatenate([value, key], axis=1), right)
     dk = dk.astype(F32) + product[:, :width]
     dv = dv.astype(F32) + product[:, width:]
-    return dq.astype(BF16), dk.astype(BF16), dv.astype(BF16)
+    return dk.astype(BF16), dv.astype(BF16)
 
 
 def own_half_kernel(
@@ -266,42 +261,51 @@
         widen(lam_ref, first_row, slice(c * tile, (c + 1) * tile), wide_ref)
         for i in range(half):
             h = start + i
-            dq_ref[c, h], dk_ref[c, h], dv_ref[c, h] = add_received(
-                half_ref[i], gin_ref[c, h] + state_ref[i], wide_ref,
-                k_ref[c, h], v_ref[c, h], g_ref[c, h],
-                dq_in[c, h], dk_in[c, h], dv_in[c, h],
+            dq_ref[c, h] = add_to_query(half_ref[i], wide_ref, g_ref[c, h], dq_in[c, h])
+            dk_ref[c, h], dv_ref[c, h] = add_to_key_value(
+                gin_ref[c, h] + state_ref[i], k_ref[c, h], v_ref[c, h], dk_in[c, h], dv_in[c, h]
             )
 
 
 def final_kernel(
     first_row, flag_ref, lam_ref, k_ref, v_ref, g_ref, dq_in, dk_in, dv_in, gin_ref, sums_ref,
-    dq_ref, dk_ref, dv_ref, wide_ref, half_ref, state_ref,
+    dq_out, dk_out, dv_out, done_ref, wide_ref, half_ref, state_ref, sems,
 ):
-    heads = k_ref.shape[1]
+    chunks, heads, tile, _ = k_ref.shape
     half = half_ref.shape[0]
-
-    @pl.when(pl.program_id(0) == 0)
-    def _():
-        for i in range(half):
-            half_ref[i], state_ref[i] = received(flag_ref, sums_ref, i)
-
-    widen(lam_ref, first_row, slice(None), wide_ref)
+    outs = (dq_out, dk_out, dv_out)
+
+    def ship(n, c):
+        place = pl.ds(c * tile, tile)
+        return pltpu.make_async_copy(done_ref.at[n, c], outs[n].at[place], sems.at[n, c])
+
+    for i in range(half):
+        half_ref[i], state_ref[i] = received(flag_ref, sums_ref, i)
     for core in range(2):
 
         @pl.when(flag_ref[0] == core)
         def _():
-            done = []
-            for h in range(heads):
-                parts = [x[0, h] for x in (dq_in, dk_in, dv_in)]
-                if h // half != core:
-                    i = h % half
-                    parts = add_received(
-                        half_ref[i], gin_ref[0, h] + state_ref[i], wide_ref,
-                        k_ref[0, h], v_ref[0, h], g_ref[0, h], *parts,
-                    )
-                done.append(parts)
-            for out_ref, parts in zip((dq_ref, dk_ref, dv_ref), zip(*done)):
-                out_ref[...] = jnp.swapaxes(jnp.stack(parts), 0, 1)
+            for c in range(chunks):
+                widen(lam_ref, first_row, slice(c * tile, (c + 1) * tile), wide_ref)
+                queries, keys, values = [], [], []
+                for h in range(heads):
+                    query, key, value = dq_in[c, h], dk_in[c, h], dv_in[c, h]
+                    if h // half != core:
+                        i = h % half
+                        query = add_to_query(half_ref[i], wide_ref, g_ref[c, h], query)
+                        key, value = add_to_key_value(
+                            gin_ref[c, h] + state_ref[i], k_ref[c, h], v_ref[c, h], key, value
+                        )
+                    queries.append(query)
+                    keys.append(key)
+                    values.append(value)
+                for n, parts in enumerate((queries, keys, values)):
+                    done_ref[n, c] = jnp.swapaxes(jnp.stack(parts), 0, 1)
+                    ship(n, c).start()
+
+    for c in range(chunks):
+        for n in range(3):
+            ship(n, c).wait()
 
 
 def shape(dims, dtype):
@@ -356,30 +360,24 @@
     square = (width, width)
     size = count * heads * width
     groups_in = len(level_sources(chunks))
-    queries, out_grad = [x.reshape(chunks, tile, heads, width) for x in (queries, out_grad)]
     queries, keys, values, out_grad = in_hbm(queries, keys, values, out_grad)
 
-    kh, vh, level_state, state, queries, out_grad = pl.pallas_call(
+    kh, vh, level_state, state = pl.pallas_call(
         states_kernel,
         grid=(chunks,),
-        in_specs=[token_block, token_block, anywhere, anywhere],
+        in_specs=[token_block, token_block],
         out_specs=[
             head_block, head_block, whole(groups_in, heads, *square), whole(heads, *square),
-            in_vmem, in_vmem,
         ],
         out_shape=[
             natural, natural, pltpu.VMEM((groups_in, heads, *square), BF16),
             pltpu.VMEM((heads, *square), F32),
-            *[pltpu.VMEM((chunks, tile, heads, width), BF16)] * 2,
-        ],
-        scratch_shapes=[
-            pltpu.VMEM((chunks, heads, *square), F32),
-            pltpu.SemaphoreType.DMA((2, chunks)),
-        ],
+        ],
+        scratch_shapes=[pltpu.VMEM((chunks, heads, *square), F32)],
         compiler_params=params(10),
         cost_estimate=cost(2 * size * width, 8 * size),
         name="states",
-    )(keys, values, queries, out_grad)
+    )(keys, values)
 
     group = lax.axis_index("head")
     pieces = [
@@ -399,12 +397,16 @@
     factor = jnp.exp2(-0.5 * jnp.maximum(order.astype(F32) - 1.0, 0.0)) / 16.0
     on_bit = jnp.bitwise_and(jnp.right_shift(here, jnp.maximum(order - local_bits - 1, 0)), 1)
     factor = jnp.where(order > local_bits, factor * on_bit.astype(F32), factor)
-    lam = codes.astype(F32) * (scale * factor)[:, None]
+    codes, factor = codes.astype(F32), scale * factor
+    lam = codes * factor[:, None]
 
     qh, gh, send, keep = pl.pallas_call(
-        functools.partial(grads_kernel, local_bits + 1),
+        grads_kernel,
         grid=(chunks,),
-        in_specs=[in_smem, lam_block, *[chunk_block(tile, heads, width)] * 2, whole(heads, *square)],
+        in_specs=[
+            in_smem, in_smem, pl.BlockSpec((tree_bits, tile), lambda c: (0, c)),
+            token_block, token_block, whole(heads, *square),
+        ],
         out_specs=[
             head_block, head_block,
             whole(heads + tree_bits * half, *square), whole(tree_bits * half, *square),
@@ -418,7 +420,7 @@
         compiler_params=params(10),
         cost_estimate=cost(2 * tree_bits * size * width, 8 * size),
         name="level_grads",
-    )(flags, lam, *near(queries, out_grad, state))
+    )(flags, factor[local_bits + 1 :], codes[local_bits + 1 :], queries, out_grad, *near(state))
     found = permute(send, 1)
     kh, vh, qh, gh, level_state, keep = near(kh, vh, qh, gh, level_state, keep)
 
@@ -432,20 +434,19 @@
         cost_estimate=cost(14 * size * tile / chunks, 4 * size),
         name="first_tile",
     )(lam, kh, vh, qh, gh)
+    hops = [1 << b | m for b in range(1, tree_bits) for m in range(0, 1 << b, 2)]
+    hops.sort(key=lambda hop: (hop & hop - 1) == 0)
     messages = pl.pallas_call(
-        pair_kernel,
+        functools.partial(pair_kernel, [bits_of(hop) for hop in hops]),
         in_specs=[in_smem, in_vmem, in_vmem],
-        out_specs=[in_vmem] * (tree_bits - 1),
-        out_shape=[pltpu.VMEM((half, *square), F32)] * (tree_bits - 1),
+        out_specs=[in_vmem] * len(hops),
+        out_shape=[pltpu.VMEM((half, *square), F32)] * len(hops),
         compiler_params=params(4),
         cost_estimate=cost(size, size),
         name="pair",
     )(flags, keep, found)
     *messages, parts = lax.optimization_barrier((*messages, parts))
-    arrived = [
-        [permute(messages[b - 1], 1 << b | m) for m in range(0, 1 << b, 2)]
-        for b in range(1, tree_bits)
-    ]
+    arrived = [permute(x, hop) for hop, x in zip(hops, messages)]
     *parts, gin = pl.pallas_call(
         local_kernel,
         in_specs=[in_smem] + [in_vmem] * 8 + [anywhere] * 3,
@@ -458,17 +459,16 @@
         name="local",
     )(flags, lam, kh, vh, qh, gh, level_state, found, *near(dqt, *parts))
     arrived, parts = lax.optimization_barrier((arrived, parts))
-    flat = [x for some in arrived for x in some]
     sums_shape = (tree_bits - 1, half, *square)
     mine = pl.pallas_call(
-        functools.partial(sum_kernel, [len(some) for some in arrived]),
-        in_specs=[in_vmem] * len(flat),
+        functools.partial(sum_kernel, [bits_of(hop) for hop in hops]),
+        in_specs=[in_vmem] * len(hops),
         out_specs=in_vmem,
         out_shape=pltpu.VMEM(sums_shape, F32),
         compiler_params=params(6),
         cost_estimate=cost(size, size),
         name="sums",
-    )(*flat)
+    )(*arrived)
     others = permute(mine, 1)
 
     kept = [
@@ -491,13 +491,13 @@
     others, parts = lax.optimization_barrier((others, parts))
     return pl.pallas_call(
         functools.partial(final_kernel, local_bits + 2),
-        grid=(chunks,),
-        in_specs=[
-            in_smem, lam_block, *[head_block] * 6, chunk_block(heads, *square), whole(*sums_shape),
-        ],
-        out_specs=[token_block] * 3,
-        out_shape=[shape((count, heads, width), BF16)] * 3,
-        scratch_shapes=kept,
+        in_specs=[in_smem] + [in_vmem] * 9,
+        out_specs=[anywhere] * 3,
+        out_shape=[pltpu.HBM((count, heads, width), BF16)] * 3,
+        scratch_shapes=[
+            pltpu.VMEM((3, chunks, tile, heads, width), BF16), *kept,
+            pltpu.SemaphoreType.DMA((3, chunks)),
+        ],
         compiler_params=params(12),
         cost_estimate=cost((tree_bits + 2) * size * width, 16 * size),
         name="final",

time: 44.8 us -> 42.6 us (0.951)
  Pallas kernels: 30 us -> 28.8 us
  starting transfers between devices: 10.7 us -> 9.81 us
    pallas_call x1, Pallas kernels: 5.43 us -> 4.01 us  [on_device(): pl.pallas_call(states_kernel, grid=(chunks,), in_specs=[token_block, toke...]
    ppermute x3, starting transfers between devices: 7.01 us -> 6.11 us  [on_device(): lax.ppermute(level_codes, 'head', [(i, (i + r) % groups) for i in range(g...]
  transfers between devices with their start and end apart: 8 -> 8, of which waited for: 2 -> 2; matrix products, arithmetic and copies ran while one was open for 0% -> 0% of each run, Pallas kernels for 43% -> 42%
where the time goes in v1:
time: 42.6 us; the launch traced here: 42.3 us
  Pallas kernels  28.8 us (68%)
  starting transfers between devices  9.81 us (23%)
  waiting for transfers between devices  2.56 us (6%)
  between operations  0.94 us (2%)
    pallas_call x1, Pallas kernels, on_device(): pl.pallas_call(local_kernel, in_specs=[in_smem] + [in_vmem] * 8 + [anywhe...  9.69 us
    ppermute x3, starting transfers between devices, on_device(): lax.ppermute(level_codes, 'head', [(i, (i + r) % groups) for i in range(g...  6.11 us
    pallas_call x1, Pallas kernels, on_device(): pl.pallas_call(functools.partial(final_kernel, local_bits + 2), in_specs=...  5.51 us
    pallas_call x1, Pallas kernels, on_device(): pl.pallas_call(grads_kernel, grid=(chunks,), in_specs=[in_smem, in_smem,...  4.75 us
    pallas_call x1, Pallas kernels, on_device(): pl.pallas_call(states_kernel, grid=(chunks,), in_specs=[token_block, toke...  4.01 us
    ppermute x5, starting transfers between devices, permute(): return lax.ppermute(x, 'seq', [(i, i ^ apart) for i in range(blocks)])  3.7 us
    ppermute x5, waiting for transfers between devices, permute(): return lax.ppermute(x, 'seq', [(i, i ^ apart) for i in range(blocks)])  2.55 us
    pallas_call x1, Pallas kernels, on_device(): pl.pallas_call(first_tile_kernel, in_specs=[in_vmem] * 5, out_specs=[in_v...  2.16 us
  transfers between devices with their start and end apart: 8, of which 2 were waited for; matrix products, arithmetic and copies ran while one was open for 0% of the time, Pallas kernels for 42%

profile of v1, /device:TPU:0, one launch (start us, length us, event | category | flops | bytes accessed | tf_op | source)
XLA Modules:
  0.0 42.3 jit_solution(8433473108996894627)
XLA Ops:
  0.6 3.1 %collective-permute-start = (s32[21,256]{1,0:T(8,128)}, s32[21,256]{1,0:T(8,128)S(1)}, u32[]{:S(2)}, u32[]{:S(2)}) collective-permute-start(s32[21,256]{1,0:T(8,128)} %param.9), channel_id=1, source_target_pairs={{0,1},{1,2},{2,3},{3,0},{4,5},{5,6},{6,7},{7,4},{8,9},{9,10},{10,1... | collective-permute-start | bytes 64520 | tf_op jit(solution)/shard_map/ppermute | solution.py:384
  3.7 2.1 %collective-permute-start.2 = (s32[21,256]{1,0:T(8,128)}, s32[21,256]{1,0:T(8,128)S(1)}, u32[]{:S(2)}, u32[]{:S(2)}) collective-permute-start(s32[21,256]{1,0:T(8,128)} %param.9), channel_id=1, source_target_pairs={{0,3},{1,0},{2,1},{3,2},{4,7},{5,4},{6,5},{7,6},{8,11},{9,8},{10,9... | collective-permute-start | bytes 64520 | tf_op jit(solution)/shard_map/ppermute | solution.py:384
  5.8 0.9 %collective-permute-start.1 = (s32[21,256]{1,0:T(8,128)}, s32[21,256]{1,0:T(8,128)S(1)}, u32[]{:S(2)}, u32[]{:S(2)}) collective-permute-start(s32[21,256]{1,0:T(8,128)} %param.9), channel_id=1, source_target_pairs={{0,2},{1,3},{2,0},{3,1},{4,6},{5,7},{6,4},{7,5},{8,10},{9,11},{10,... | collective-permute-start | bytes 64520 | tf_op jit(solution)/shard_map/ppermute | solution.py:384
  6.8 0.1 slice.38.factor_ref
  6.8 0.0 copy-start
  6.8 4.0 %states.1 = (bf16[4,8,256,128]{3,2,1,0:T(8,128)(2,1)S(1)}, bf16[4,8,256,128]{3,2,1,0:T(8,128)(2,1)S(1)}, bf16[3,8,128,128]{3,2,1,0:T(8,128)(2,1)S(1)}, f32[8,128,128]{2,1,0:T(8,128)S(1)}) custom-call(bf16[1024,8,128]{2,1,0:T(8,128)(2,1)} %k_ref.1, bf16[1024,8,128]{2,1,0:T(8,128)(2,1)} %v_ref.1), custom_call_target="tpu_custom_call" | custom-call | flops 268435456 | bytes 8388608 | tf_op jit(solution)/shard_map/states/pallas_call | solution.py:365
  10.9 0.0 collective-permute-done
  10.9 0.0 collective-permute-done.2
  10.9 0.0 collective-permute-done.1
  10.9 0.0 copy-done
  11.0 4.8 %level_grads.1 = (bf16[4,8,256,128]{3,2,1,0:T(8,128)(2,1)S(1)}, bf16[4,8,256,128]{3,2,1,0:T(8,128)(2,1)S(1)}, f32[20,128,128]{2,1,0:T(8,128)S(1)}, f32[12,128,128]{2,1,0:T(8,128)S(1)}) custom-call(s32[3]{0:T(128)S(1)} %shift-right-arithmetic_and_fusion.flag_ref, f32[3]{0:T(128)S(1)} %slice.38.factor_ref, f32[3,1024]{1,0:T(4,128)S(1)} %slice.40.codes_ref, ...), custom_call_target="tpu_custom_call" | custom-call | flops 805306368 | bytes 8388608 | tf_op jit(solution)/shard_map/level_grads/pallas_call | solution.py:403
  15.7 0.1 collective-permute-start.3
  15.8 0.1 broadcast_multiply_fusion.lam_ref
  15.9 2.2 %first_tile.1 = (f32[8,128,256]{2,1,0:T(8,128)S(1)}, bf16[4,8,256,128]{3,2,1,0:T(8,128)(2,1)S(1)}, bf16[4,8,256,128]{3,2,1,0:T(8,128)(2,1)S(1)}, bf16[4,8,256,128]{3,2,1,0:T(8,128)(2,1)S(1)}) custom-call(f32[14,1024]{1,0:T(8,128)S(1)} %broadcast_multiply_fusion.lam_ref, bf16[4,8,256,128]{3,2,1,0:T(8,128)(2,1)S(1)} %get-tuple-element.49.k_ref, ...), custom_call_target="tpu_custom_call" | custom-call | flops 939524096 | bytes 4194304 | tf_op jit(solution)/shard_map/first_tile/pallas_call | solution.py:427
  18.1 0.8 %collective-permute-done.3.found_ref = f32[20,128,128]{2,1,0:T(8,128)S(1)} collective-permute-done((f32[20,128,128]{2,1,0:T(8,128)S(1)}, f32[20,128,128]{2,1,0:T(8,128)S(1)}, u32[]{:S(2)}, u32[]{:S(2)}) %collective-permute-start.3) | collective-permute-done | bytes 1310752 | tf_op jit(solution)/shard_map/ppermute | solution.py:338
  18.8 0.7 %pair.1 = (f32[4,128,128]{2,1,0:T(8,128)S(1)}, f32[4,128,128]{2,1,0:T(8,128)S(1)}, f32[4,128,128]{2,1,0:T(8,128)S(1)}) custom-call(s32[3]{0:T(128)S(1)} %shift-right-arithmetic_and_fusion.flag_ref, f32[12,128,128]{2,1,0:T(8,128)S(1)} %get-tuple-element.53.keep_ref, f32[20,128,128]{2,1,0:T(8,128)S(1)} %collective-permute-done.3.found_ref), custom_call_target="tpu_custom_call" | custom-call | flops 1048576 | bytes 1048576 | tf_op jit(solution)/shard_map/pair/pallas_call | solution.py:439
  19.5 2.5 %collective-permute-start.4 = (f32[4,128,128]{2,1,0:T(8,128)S(1)}, f32[4,128,128]{2,1,0:T(8,128)S(1)}, u32[]{:S(2)}, u32[]{:S(2)}) collective-permute-start(f32[4,128,128]{2,1,0:T(8,128)S(1)} %get-tuple-element.62), channel_id=1, source_target_pairs={{0,24},{4,28},{8,16},{12,20},{16,8},{20,12},{24,0},{28,4},{1,25},{... | collective-permute-start | bytes 786440 | tf_op jit(solution)/shard_map/ppermute | solution.py:338
  22.0 0.5 %collective-permute-start.5 = (f32[4,128,128]{2,1,0:T(8,128)S(1)}, f32[4,128,128]{2,1,0:T(8,128)S(1)}, u32[]{:S(2)}, u32[]{:S(2)}) collective-permute-start(f32[4,128,128]{2,1,0:T(8,128)S(1)} %get-tuple-element.63), channel_id=1, source_target_pairs={{0,8},{4,12},{8,0},{12,4},{16,24},{20,28},{24,16},{28,20},{1,9},{5... | collective-permute-start | bytes 786440 | tf_op jit(solution)/shard_map/ppermute | solution.py:338
  22.6 0.5 %collective-permute-start.6 = (f32[4,128,128]{2,1,0:T(8,128)S(1)}, f32[4,128,128]{2,1,0:T(8,128)S(1)}, u32[]{:S(2)}, u32[]{:S(2)}) collective-permute-start(f32[4,128,128]{2,1,0:T(8,128)S(1)} %get-tuple-element.64), channel_id=1, source_target_pairs={{0,16},{4,20},{8,24},{12,28},{16,0},{20,4},{24,8},{28,12},{1,17},{... | collective-permute-start | bytes 786440 | tf_op jit(solution)/shard_map/ppermute | solution.py:338
  23.1 9.7 %local.1 = (bf16[4,8,256,128]{3,2,1,0:T(8,128)(2,1)S(1)}, bf16[4,8,256,128]{3,2,1,0:T(8,128)(2,1)S(1)}, bf16[4,8,256,128]{3,2,1,0:T(8,128)(2,1)S(1)}, f32[4,8,128,128]{3,2,1,0:T(8,128)S(1)}) custom-call(s32[3]{0:T(128)S(1)} %shift-right-arithmetic_and_fusion.flag_ref, ...), custom_call_target="tpu_custom_call", output_to_operand_aliasing={{0}: (9, {}), {1}: (10, {}), {2}: (11, {})} | custom-call | flops 3758096384 | bytes 4194304 | tf_op jit(solution)/shard_map/local/pallas_call | solution.py:450
  32.8 0.0 collective-permute-done.4.refs_0_
  32.8 1.8 %collective-permute-done.5.refs_1_ = f32[4,128,128]{2,1,0:T(8,128)S(1)} collective-permute-done((f32[4,128,128]{2,1,0:T(8,128)S(1)}, f32[4,128,128]{2,1,0:T(8,128)S(1)}, u32[]{:S(2)}, u32[]{:S(2)}) %collective-permute-start.5) | collective-permute-done | bytes 262176 | tf_op jit(solution)/shard_map/ppermute | solution.py:338
  34.5 0.0 collective-permute-done.6.refs_2_
  34.6 0.1 collective-permute-start.7
  34.7 2.0 %own_half.1 = (bf16[4,8,256,128]{3,2,1,0:T(8,128)(2,1)S(1)}, bf16[4,8,256,128]{3,2,1,0:T(8,128)(2,1)S(1)}, bf16[4,8,256,128]{3,2,1,0:T(8,128)(2,1)S(1)}) custom-call(s32[3]{0:T(128)S(1)} %shift-right-arithmetic_and_fusion.flag_ref, f32[14,1024]{1,0:T(8,128)S(1)} %broadcast_multiply_fusion.lam_ref, ...), custom_call_target="tpu_custom_call", output_to_operand_aliasing={{0}: (7, {}), {1}: (8, {}), {2}: (9, {})} | custom-call | flops 671088640 | bytes 8388608 | tf_op jit(solution)/shard_map/own_half/pallas_call | solution.py:480
  36.7 0.0 collective-permute-done.7.sums_ref
  36.7 5.5 %final.1 = (bf16[1024,8,128]{2,1,0:T(8,128)(2,1)}, bf16[1024,8,128]{2,1,0:T(8,128)(2,1)}, bf16[1024,8,128]{2,1,0:T(8,128)(2,1)}) custom-call(s32[3]{0:T(128)S(1)} %shift-right-arithmetic_and_fusion.flag_ref, f32[14,1024]{1,0:T(8,128)S(1)} %broadcast_multiply_fusion.lam_ref, bf16[4,8,256,128]{3,2,1,0:T(8,128)(2,1)S(1)} %get-tuple-element.49.k_ref, ...), custom_call_target="tpu_custom_call" | custom-call | flops 671088640 | bytes 16777216 | tf_op jit(solution)/shard_map/final/pallas_call | solution.py:492
  (7 shorter events, 0.1 us)
Async XLA Ops:
  0.6 10.2 %collective-permute-start = (s32[21,256]{1,0:T(8,128)}, s32[21,256]{1,0:T(8,128)S(1)}, u32[]{:S(2)}, u32[]{:S(2)}) collective-permute-start(s32[21,256]{1,0:T(8,128)} %param.9), channel_id=1, source_target_pairs={{0,1},{1,2},{2,3},{3,0},{4,5},{5,6},{6,7},{7,4},{8,9},{9,10},{10,1... | collective-permute-start | bytes 64520 | tf_op jit(solution)/shard_map/ppermute | solution.py:384
  3.7 7.2 %collective-permute-start.2 = (s32[21,256]{1,0:T(8,128)}, s32[21,256]{1,0:T(8,128)S(1)}, u32[]{:S(2)}, u32[]{:S(2)}) collective-permute-start(s32[21,256]{1,0:T(8,128)} %param.9), channel_id=1, source_target_pairs={{0,3},{1,0},{2,1},{3,2},{4,7},{5,4},{6,5},{7,6},{8,11},{9,8},{10,9... | collective-permute-start | bytes 64520 | tf_op jit(solution)/shard_map/ppermute | solution.py:384
  5.8 5.1 %collective-permute-start.1 = (s32[21,256]{1,0:T(8,128)}, s32[21,256]{1,0:T(8,128)S(1)}, u32[]{:S(2)}, u32[]{:S(2)}) collective-permute-start(s32[21,256]{1,0:T(8,128)} %param.9), channel_id=1, source_target_pairs={{0,2},{1,3},{2,0},{3,1},{4,6},{5,7},{6,4},{7,5},{8,10},{9,11},{10,... | collective-permute-start | bytes 64520 | tf_op jit(solution)/shard_map/ppermute | solution.py:384
  6.8 4.1 %copy-start = (s32[21,256]{1,0:T(8,128)S(1)}, s32[21,256]{1,0:T(8,128)}, u32[]{:S(2)}) copy-start(s32[21,256]{1,0:T(8,128)} %param.9) | copy-start | bytes 64516
  15.7 3.1 %collective-permute-start.3 = (f32[20,128,128]{2,1,0:T(8,128)S(1)}, f32[20,128,128]{2,1,0:T(8,128)S(1)}, u32[]{:S(2)}, u32[]{:S(2)}) collective-permute-start(f32[20,128,128]{2,1,0:T(8,128)S(1)} %get-tuple-element.54), channel_id=1, source_target_pairs={{0,4},{4,0},{8,12},{12,8},{16,20},{20,16},{24,28},{28,24},{1,5},{5... | collective-permute-start | bytes 3932168 | tf_op jit(solution)/shard_map/ppermute | solution.py:338
  19.5 13.3 %collective-permute-start.4 = (f32[4,128,128]{2,1,0:T(8,128)S(1)}, f32[4,128,128]{2,1,0:T(8,128)S(1)}, u32[]{:S(2)}, u32[]{:S(2)}) collective-permute-start(f32[4,128,128]{2,1,0:T(8,128)S(1)} %get-tuple-element.62), channel_id=1, source_target_pairs={{0,24},{4,28},{8,16},{12,20},{16,8},{20,12},{24,0},{28,4},{1,25},{... | collective-permute-start | bytes 786440 | tf_op jit(solution)/shard_map/ppermute | solution.py:338
  22.0 12.5 %collective-permute-start.5 = (f32[4,128,128]{2,1,0:T(8,128)S(1)}, f32[4,128,128]{2,1,0:T(8,128)S(1)}, u32[]{:S(2)}, u32[]{:S(2)}) collective-permute-start(f32[4,128,128]{2,1,0:T(8,128)S(1)} %get-tuple-element.63), channel_id=1, source_target_pairs={{0,8},{4,12},{8,0},{12,4},{16,24},{20,28},{24,16},{28,20},{1,9},{5... | collective-permute-start | bytes 786440 | tf_op jit(solution)/shard_map/ppermute | solution.py:338
  22.6 12.0 %collective-permute-start.6 = (f32[4,128,128]{2,1,0:T(8,128)S(1)}, f32[4,128,128]{2,1,0:T(8,128)S(1)}, u32[]{:S(2)}, u32[]{:S(2)}) collective-permute-start(f32[4,128,128]{2,1,0:T(8,128)S(1)} %get-tuple-element.64), channel_id=1, source_target_pairs={{0,16},{4,20},{8,24},{12,28},{16,0},{20,4},{24,8},{28,12},{1,17},{... | collective-permute-start | bytes 786440 | tf_op jit(solution)/shard_map/ppermute | solution.py:338
  34.6 2.1 %collective-permute-start.7 = (f32[2,4,128,128]{3,2,1,0:T(8,128)S(1)}, f32[2,4,128,128]{3,2,1,0:T(8,128)S(1)}, u32[]{:S(2)}, u32[]{:S(2)}) collective-permute-start(f32[2,4,128,128]{3,2,1,0:T(8,128)S(1)} %sums.1.sums_ref), channel_id=1, source_target_pairs={{0,4},{4,0},{8,12},{12,8},{16,20},{20,16},{24,28},{28,24},{1,5},{5... | collective-permute-start | bytes 1572872 | tf_op jit(solution)/shard_map/ppermute | solution.py:338

commit v2 on v1

--- a/solution.py
+++ b/solution.py
@@ -38,6 +38,10 @@
         for first in range(0, chunks, 2 << j):
             found.append(range(first, first + (1 << j)))
     return found
+
+
+def bit_of_block(b):
+    return jnp.bitwise_and(jnp.right_shift(lax.axis_index("seq"), b), 1)
 
 
 def states_kernel(k_ref, v_ref, kh_ref, vh_ref, level_ref, total_ref, chunk_ref):
@@ -60,21 +64,19 @@
 
 
 def grads_kernel(
-    flag_ref, factor_ref, codes_ref, q_ref, g_ref, state_ref,
-    qh_ref, gh_ref, send_ref, keep_ref, grad_ref,
+    first_row, lam_ref, q_ref, g_ref, state_ref, gh_ref, qt_ref, send_ref, keep_ref, grad_ref
 ):
     heads, width = q_ref.shape[1:]
     half = heads // 2
-    levels, tile = codes_ref.shape
-    qh_ref[0] = jnp.swapaxes(q_ref[...], 0, 1)
+    levels = grad_ref.shape[0]
+    queries = jnp.swapaxes(q_ref[...], 0, 1)
     gh_ref[0] = jnp.swapaxes(g_ref[...], 0, 1)
     first = pl.program_id(0) == 0
-    rows = [
-        jnp.broadcast_to(codes_ref[b : b + 1, :], (width, tile)).astype(BF16) for b in range(levels)
-    ]
+    rows = [lam_ref[first_row + b : first_row + b + 1, :] for b in range(levels)]
     for h in range(heads):
-        query_t = qh_ref[0, h].T
-        weighted = stack_levels([row * query_t for row in rows], 0)
+        query_t = queries[h].T
+        qt_ref[0, h] = query_t
+        weighted = stack_levels([scaled(row, query_t) for row in rows], 0)
         grad = dot(weighted, gh_ref[0, h])
         for b in range(levels):
             part = grad[b * width : (b + 1) * width]
@@ -82,20 +84,16 @@
 
     for core in range(2):
 
-        @pl.when((pl.program_id(0) == pl.num_programs(0) - 1) & (flag_ref[0] == core))
+        @pl.when((pl.program_id(0) == pl.num_programs(0) - 1) & (bit_of_block(0) == core))
         def _():
             for h in range(heads):
-                send_ref[h] = state_ref[h] if core == 0 else factor_ref[0] * grad_ref[0, h]
+                send_ref[h] = state_ref[h] if core == 0 else grad_ref[0, h]
             for level in range(levels):
                 for i in range(half):
                     spot = level * half + i
-                    mine, other = core * half + i, (1 - core) * half + i
-                    if level == 0:
-                        keep_ref[spot] = state_ref[mine]
-                        send_ref[heads + spot] = state_ref[other]
-                    else:
-                        keep_ref[spot] = factor_ref[level] * grad_ref[level, mine]
-                        send_ref[heads + spot] = factor_ref[level] * grad_ref[level, other]
+                    source = state_ref if level == 0 else grad_ref.at[level]
+                    keep_ref[spot] = source[core * half + i]
+                    send_ref[heads + spot] = source[(1 - core) * half + i]
 
 
 def make_mask(lam_ref, span, mask_ref):
@@ -119,16 +117,16 @@
                 mask_ref[at : at + part, to : to + part] = jnp.zeros((part, part), F32)
 
 
-def diagonal_tile(key, value, query, grad, mask):
+def diagonal_tile(key, value, query_t, grad, mask):
     weight_q = (mask * dot_nt(value, grad)).astype(BF16)
-    weight_v = (mask * dot_nt(key, query)).astype(BF16)
-    dk = dot(weight_q, query).astype(BF16)
+    weight_v = (mask * dot(key, query_t)).astype(BF16)
+    dk = dot_nt(weight_q, query_t).astype(BF16)
     dv = dot(weight_v, grad).astype(BF16)
     return dot(key.T, weight_q), dk, dv
 
 
 def first_tile_kernel(
-    lam_ref, k_ref, v_ref, q_ref, g_ref, dqt_ref, dq_ref, dk_ref, dv_ref, mask_ref
+    lam_ref, k_ref, v_ref, qt_ref, g_ref, dqt_ref, dq_ref, dk_ref, dv_ref, mask_ref
 ):
     del dq_ref
     make_mask(lam_ref, slice(0, mask_ref.shape[0]), mask_ref)
@@ -136,12 +134,13 @@
     @pl.loop(0, k_ref.shape[1], unroll=4)
     def _(h):
         dqt_ref[h], dk_ref[0, h], dv_ref[0, h] = diagonal_tile(
-            k_ref[0, h], v_ref[0, h], q_ref[0, h], g_ref[0, h], mask_ref[...]
+            k_ref[0, h], v_ref[0, h], qt_ref[0, h], g_ref[0, h], mask_ref[...]
         )
 
 
 def local_kernel(
-    flag_ref, lam_ref, k_ref, v_ref, q_ref, g_ref, level_ref, found_ref, dqt_ref, dq_in, dk_in, dv_in,
+    lam_ref, k_ref, v_ref, qt_ref, g_ref, level_ref, found_ref, dqt_ref,
+    dq_in, dk_in, dv_in,
     dq_ref, dk_ref, dv_ref, gin_ref, mask_ref, half_ref,
 ):
     del dq_in, dk_in, dv_in
@@ -149,7 +148,7 @@
     tile_bits = bits_of(tile)
     first_row = tile_bits + bits_of(chunks) + 1
     groups = level_sources(chunks)
-    off = (1 - flag_ref[0]).astype(F32)
+    off = (1 - bit_of_block(0)).astype(F32)
 
     @pl.loop(0, heads, unroll=4)
     def _(h):
@@ -167,12 +166,11 @@
 
         @pl.loop(0, heads, unroll=4)
         def _(h):
-            query, grad = q_ref[c, h], g_ref[c, h]
+            query_t, grad = qt_ref[c, h], g_ref[c, h]
             dqt, dk_ref[c, h], dv_ref[c, h] = diagonal_tile(
-                k_ref[c, h], v_ref[c, h], query, grad, mask_ref[...]
+                k_ref[c, h], v_ref[c, h], query_t, grad, mask_ref[...]
             )
             dqt = dqt + lam_ref[first_row : first_row + 1, span] * dot_nt(half_ref[h], grad)
-            query_t = query.T
             for j in range(bits_of(chunks)):
                 if c >> j & 1:
                     row = lam_ref[tile_bits + 1 + j : tile_bits + 2 + j, span]
@@ -185,20 +183,17 @@
             dq_ref[c, h] = dqt.astype(BF16).T
 
 
-def pair_kernel(levels, flag_ref, keep_ref, found_ref, *out_refs):
+def pair_kernel(levels, keep_ref, found_ref, *out_refs):
     half = out_refs[0].shape[0]
     heads = found_ref.shape[0] - keep_ref.shape[0]
-
-    def pair(level, i):
-        return keep_ref[level * half + i] + found_ref[heads + level * half + i]
-
     for b, out_ref in zip(levels, out_refs):
         for on in range(2):
 
-            @pl.when(flag_ref[b] == on)
+            @pl.when(bit_of_block(b) == on)
             def _():
                 for i in range(half):
-                    out_ref[i] = pair(b * on, i)
+                    spot = b * on * half + i
+                    out_ref[i] = keep_ref[spot] + found_ref[heads + spot]
 
 
 def sum_kernel(levels, *refs):
@@ -215,9 +210,9 @@
         wide_ref[b] = jnp.broadcast_to(row, wide_ref.shape[:0:-1]).T
 
 
-def received(flag_ref, sums_ref, i):
+def received(sums_ref, i):
     parts = [sums_ref[b, i] for b in range(sums_ref.shape[0])]
-    off = [(1 - flag_ref[b + 1]).astype(F32) for b in range(len(parts))]
+    off = [(1 - bit_of_block(b + 1)).astype(F32) for b in range(len(parts))]
     state = functools.reduce(jnp.add, [w * part for w, part in zip(off, parts)])
     return stack_levels([part.astype(BF16) for part in parts], 0), state
 
@@ -249,14 +244,14 @@
 
 
 def own_half_kernel(
-    first_row, flag_ref, lam_ref, k_ref, v_ref, g_ref, gin_ref, sums_ref, dq_in, dk_in, dv_in,
+    first_row, lam_ref, k_ref, v_ref, g_ref, gin_ref, sums_ref, dq_in, dk_in, dv_in,
     dq_ref, dk_ref, dv_ref, wide_ref, half_ref, state_ref,
 ):
     chunks, _, tile, _ = k_ref.shape
     half = half_ref.shape[0]
-    start = flag_ref[0] * half
+    start = bit_of_block(0) * half
     for i in range(half):
-        half_ref[i], state_ref[i] = received(flag_ref, sums_ref, i)
+        half_ref[i], state_ref[i] = received(sums_ref, i)
     for c in range(chunks):
         widen(lam_ref, first_row, slice(c * tile, (c + 1) * tile), wide_ref)
         for i in range(half):
@@ -268,7 +263,7 @@
 
 
 def final_kernel(
-    first_row, flag_ref, lam_ref, k_ref, v_ref, g_ref, dq_in, dk_in, dv_in, gin_ref, sums_ref,
+    first_row, lam_ref, k_ref, v_ref, g_ref, dq_in, dk_in, dv_in, gin_ref, sums_ref,
     dq_out, dk_out, dv_out, done_ref, wide_ref, half_ref, state_ref, sems,
 ):
     chunks, heads, tile, _ = k_ref.shape
@@ -280,10 +275,10 @@
         return pltpu.make_async_copy(done_ref.at[n, c], outs[n].at[place], sems.at[n, c])
 
     for i in range(half):
-        half_ref[i], state_ref[i] = received(flag_ref, sums_ref, i)
+        half_ref[i], state_ref[i] = received(sums_ref, i)
     for core in range(2):
 
-        @pl.when(flag_ref[0] == core)
+        @pl.when(bit_of_block(0) == core)
         def _():
             for c in range(chunks):
                 widen(lam_ref, first_row, slice(c * tile, (c + 1) * tile), wide_ref)
@@ -332,7 +327,6 @@
     chunks = count // tile
     half = heads // 2
     rows = local_bits + 1 + tree_bits
-    flags = jnp.bitwise_and(jnp.right_shift(here, jnp.arange(max(tree_bits, 1))), 1)
 
     def permute(x, apart):
         return lax.ppermute(x, "seq", [(i, i ^ apart) for i in range(blocks)])
@@ -344,8 +338,6 @@
         return [pltpu.with_memory_space_constraint(x, pltpu.VMEM) for x in arrays]
 
     token_block = pl.BlockSpec((tile, heads, width), lambda c: (c, 0, 0))
-    lam_block = pl.BlockSpec((rows, tile), lambda c: (0, c))
-    in_smem = pl.BlockSpec(memory_space=pltpu.SMEM)
     in_vmem = pl.BlockSpec(memory_space=pltpu.VMEM)
     anywhere = pl.BlockSpec(memory_space=pl.ANY)
 
@@ -374,21 +366,21 @@
             pltpu.VMEM((heads, *square), F32),
         ],
         scratch_shapes=[pltpu.VMEM((chunks, heads, *square), F32)],
-        compiler_params=params(10),
+        compiler_params=params(8),
         cost_estimate=cost(2 * size * width, 8 * size),
         name="states",
     )(keys, values)
 
     group = lax.axis_index("head")
     pieces = [
-        lax.ppermute(level_codes, "head", [(i, (i + r) % groups) for i in range(groups)])
+        lax.ppermute(level_codes, "head", [(i, i ^ r) for i in range(groups)])
         for r in range(1, groups)
     ]
     pieces, state = lax.optimization_barrier((pieces, state))
     pieces = jnp.stack([level_codes, *pieces])
     codes = jnp.concatenate(
         [
-            lax.dynamic_index_in_dim(pieces, (group - j) % groups, 0, keepdims=False)[:rows]
+            lax.dynamic_index_in_dim(pieces, jnp.bitwise_xor(group, j), 0, keepdims=False)[:rows]
             for j in range(groups)
         ],
         axis=1,
@@ -397,32 +389,31 @@
     factor = jnp.exp2(-0.5 * jnp.maximum(order.astype(F32) - 1.0, 0.0)) / 16.0
     on_bit = jnp.bitwise_and(jnp.right_shift(here, jnp.maximum(order - local_bits - 1, 0)), 1)
     factor = jnp.where(order > local_bits, factor * on_bit.astype(F32), factor)
-    codes, factor = codes.astype(F32), scale * factor
-    lam = codes * factor[:, None]
-
-    qh, gh, send, keep = pl.pallas_call(
-        grads_kernel,
+    lam = codes.astype(F32) * (scale * factor)[:, None]
+
+    gh, qt, send, keep = pl.pallas_call(
+        functools.partial(grads_kernel, local_bits + 1),
         grid=(chunks,),
         in_specs=[
-            in_smem, in_smem, pl.BlockSpec((tree_bits, tile), lambda c: (0, c)),
-            token_block, token_block, whole(heads, *square),
+            pl.BlockSpec((rows, tile), lambda c: (0, c)), token_block, token_block,
+            whole(heads, *square),
         ],
         out_specs=[
-            head_block, head_block,
+            head_block, chunk_block(heads, width, tile),
             whole(heads + tree_bits * half, *square), whole(tree_bits * half, *square),
         ],
         out_shape=[
-            natural, natural,
+            natural, pltpu.VMEM((chunks, heads, width, tile), BF16),
             pltpu.VMEM((heads + tree_bits * half, *square), F32),
             pltpu.VMEM((tree_bits * half, *square), F32),
         ],
         scratch_shapes=[pltpu.VMEM((tree_bits, heads, *square), F32)],
-        compiler_params=params(10),
+        compiler_params=params(8),
         cost_estimate=cost(2 * tree_bits * size * width, 8 * size),
         name="level_grads",
-    )(flags, factor[local_bits + 1 :], codes[local_bits + 1 :], queries, out_grad, *near(state))
+    )(lam, queries, out_grad, *near(state))
     found = permute(send, 1)
-    kh, vh, qh, gh, level_state, keep = near(kh, vh, qh, gh, level_state, keep)
+    kh, vh, qt, gh, level_state, keep = near(kh, vh, qt, gh, level_state, keep)
 
     dqt, *parts = pl.pallas_call(
         first_tile_kernel,
@@ -430,34 +421,34 @@
         out_specs=[in_vmem] * 4,
         out_shape=[pltpu.VMEM((heads, width, tile), F32)] + [natural] * 3,
         scratch_shapes=[pltpu.VMEM((tile, tile), F32)],
-        compiler_params=params(6),
+        compiler_params=params(3),
         cost_estimate=cost(14 * size * tile / chunks, 4 * size),
         name="first_tile",
-    )(lam, kh, vh, qh, gh)
+    )(lam, kh, vh, qt, gh)
     hops = [1 << b | m for b in range(1, tree_bits) for m in range(0, 1 << b, 2)]
     hops.sort(key=lambda hop: (hop & hop - 1) == 0)
     messages = pl.pallas_call(
         functools.partial(pair_kernel, [bits_of(hop) for hop in hops]),
-        in_specs=[in_smem, in_vmem, in_vmem],
+        in_specs=[in_vmem] * 2,
         out_specs=[in_vmem] * len(hops),
         out_shape=[pltpu.VMEM((half, *square), F32)] * len(hops),
-        compiler_params=params(4),
+        compiler_params=params(2),
         cost_estimate=cost(size, size),
         name="pair",
-    )(flags, keep, found)
+    )(keep, found)
     *messages, parts = lax.optimization_barrier((*messages, parts))
     arrived = [permute(x, hop) for hop, x in zip(hops, messages)]
     *parts, gin = pl.pallas_call(
         local_kernel,
-        in_specs=[in_smem] + [in_vmem] * 8 + [anywhere] * 3,
+        in_specs=[in_vmem] * 8 + [anywhere] * 3,
         out_specs=[in_vmem] * 4,
         out_shape=[natural] * 3 + [pltpu.VMEM((chunks, heads, *square), F32)],
-        input_output_aliases={9: 0, 10: 1, 11: 2},
+        input_output_aliases={8: 0, 9: 1, 10: 2},
         scratch_shapes=[pltpu.VMEM((tile, tile), F32), pltpu.VMEM((heads, *square), BF16)],
-        compiler_params=params(6),
+        compiler_params=params(3),
         cost_estimate=cost(14 * size * tile, 4 * size),
         name="local",
-    )(flags, lam, kh, vh, qh, gh, level_state, found, *near(dqt, *parts))
+    )(lam, kh, vh, qt, gh, level_state, found, *near(dqt, *parts))
     arrived, parts = lax.optimization_barrier((arrived, parts))
     sums_shape = (tree_bits - 1, half, *square)
     mine = pl.pallas_call(
@@ -465,7 +456,7 @@
         in_specs=[in_vmem] * len(hops),
         out_specs=in_vmem,
         out_shape=pltpu.VMEM(sums_shape, F32),
-        compiler_params=params(6),
+        compiler_params=params(2),
         cost_estimate=cost(size, size),
         name="sums",
     )(*arrived)
@@ -479,29 +470,29 @@
     gin, mine = near(gin, mine)
     parts = pl.pallas_call(
         functools.partial(own_half_kernel, local_bits + 2),
-        in_specs=[in_smem] + [in_vmem] * 9,
+        in_specs=[in_vmem] * 9,
         out_specs=[in_vmem] * 3,
         out_shape=[natural] * 3,
-        input_output_aliases={7: 0, 8: 1, 9: 2},
+        input_output_aliases={6: 0, 7: 1, 8: 2},
         scratch_shapes=kept,
-        compiler_params=params(6),
+        compiler_params=params(3),
         cost_estimate=cost((tree_bits + 2) * size * width, 8 * size),
         name="own_half",
-    )(flags, lam, kh, vh, gh, gin, mine, *near(*parts))
+    )(lam, kh, vh, gh, gin, mine, *near(*parts))
     others, parts = lax.optimization_barrier((others, parts))
     return pl.pallas_call(
         functools.partial(final_kernel, local_bits + 2),
-        in_specs=[in_smem] + [in_vmem] * 9,
+        in_specs=[in_vmem] * 9,
         out_specs=[anywhere] * 3,
         out_shape=[pltpu.HBM((count, heads, width), BF16)] * 3,
         scratch_shapes=[
             pltpu.VMEM((3, chunks, tile, heads, width), BF16), *kept,
             pltpu.SemaphoreType.DMA((3, chunks)),
         ],
-        compiler_params=params(12),
+        compiler_params=params(10),
         cost_estimate=cost((tree_bits + 2) * size * width, 16 * size),
         name="final",
-    )(flags, lam, kh, vh, gh, *near(*parts), gin, others)
+    )(lam, kh, vh, gh, *near(*parts), gin, others)
 
 
 def solution(mesh):

time: 42.6 us -> 41.6 us (0.977)
  Pallas kernels: 28.8 us -> 26 us
  waiting for transfers between devices: 2.56 us -> 4.93 us
  starting transfers between devices: 9.81 us -> 9.38 us
    ppermute x5, waiting for transfers between devices: 2.55 us -> 3.93 us  [permute(): return lax.ppermute(x, 'seq', [(i, i ^ apart) for i in range(blocks)])]
    ppermute x3, waiting for transfers between devices: 0.01 us -> 1 us  [on_device(): lax.ppermute(level_codes, 'head', [(i, i ^ r) for i in range(groups)])]
    pallas_call x1, Pallas kernels: 5.51 us -> 4.65 us  [on_device(): pl.pallas_call(functools.partial(final_kernel, local_bits + 2), in_specs=...]
    pallas_call x2, Pallas kernels: 14.4 us -> 13.8 us  [the longest x1 9.01 us: on_device(): pl.pallas_call(local_kernel, in_specs=[in_vmem] * 8 + [anywhere] * 3, out...]
    pallas_call x1, Pallas kernels: 1.99 us -> 1.34 us  [on_device(): pl.pallas_call(functools.partial(own_half_kernel, local_bits + 2), in_spe...]
    pallas_call x1, Pallas kernels: 0.66 us -> 0.1 us  [on_device(): pl.pallas_call(functools.partial(pair_kernel, [bits_of(hop) for hop in ho...]
    ppermute x3, starting transfers between devices: 6.11 us -> 5.68 us  [on_device(): lax.ppermute(level_codes, 'head', [(i, i ^ r) for i in range(groups)])]
  transfers between devices with their start and end apart: 8 -> 8, of which waited for: 2 -> 4; matrix products, arithmetic and copies ran while one was open for 0% -> 0% of each run, Pallas kernels for 42% -> 40%
where the time goes in v2:
time: 41.6 us; the launch traced here: 41.4 us
  Pallas kernels  26 us (62%)
  starting transfers between devices  9.38 us (23%)
  waiting for transfers between devices  4.93 us (12%)
  between operations  0.92 us (2%)
    pallas_call x1, Pallas kernels, on_device(): pl.pallas_call(local_kernel, in_specs=[in_vmem] * 8 + [anywhere] * 3, out...  9.01 us
    ppermute x3, starting transfers between devices, on_device(): lax.ppermute(level_codes, 'head', [(i, i ^ r) for i in range(groups)])  5.68 us
    pallas_call x1, Pallas kernels, on_device(): pl.pallas_call(functools.partial(grads_kernel, local_bits + 1), grid=(chu...  4.76 us
    pallas_call x1, Pallas kernels, on_device(): pl.pallas_call(functools.partial(final_kernel, local_bits + 2), in_specs=...  4.65 us
    pallas_call x1, Pallas kernels, on_device(): pl.pallas_call(states_kernel, grid=(chunks,), in_specs=[token_block, toke...  4.02 us
    ppermute x5, waiting for transfers between devices, permute(): return lax.ppermute(x, 'seq', [(i, i ^ apart) for i in range(blocks)])  3.93 us
    ppermute x5, starting transfers between devices, permute(): return lax.ppermute(x, 'seq', [(i, i ^ apart) for i in range(blocks)])  3.7 us
    pallas_call x1, Pallas kernels, on_device(): pl.pallas_call(first_tile_kernel, in_specs=[in_vmem] * 5, out_specs=[in_v...  2.08 us
  transfers between devices with their start and end apart: 8, of which 4 were waited for; matrix products, arithmetic and copies ran while one was open for 0% of the time, Pallas kernels for 40%

profile of v2, /device:TPU:0, one launch (start us, length us, event | category | flops | bytes accessed | tf_op | source)
XLA Modules:
  0.0 41.4 jit_solution(12499834172120278791)
XLA Ops:
  0.6 3.1 %collective-permute-start = (s32[21,256]{1,0:T(8,128)}, s32[21,256]{1,0:T(8,128)S(1)}, u32[]{:S(2)}, u32[]{:S(2)}) collective-permute-start(s32[21,256]{1,0:T(8,128)} %param.9), channel_id=1, source_target_pairs={{0,1},{1,0},{2,3},{3,2},{4,5},{5,4},{6,7},{7,6},{8,9},{9,8},{10,11... | collective-permute-start | bytes 64520 | tf_op jit(solution)/shard_map/ppermute | solution.py:376
  3.7 2.5 %collective-permute-start.2 = (s32[21,256]{1,0:T(8,128)}, s32[21,256]{1,0:T(8,128)S(1)}, u32[]{:S(2)}, u32[]{:S(2)}) collective-permute-start(s32[21,256]{1,0:T(8,128)} %param.9), channel_id=1, source_target_pairs={{0,3},{1,2},{2,1},{3,0},{4,7},{5,6},{6,5},{7,4},{8,11},{9,10},{10,... | collective-permute-start | bytes 64520 | tf_op jit(solution)/shard_map/ppermute | solution.py:376
  6.2 0.1 collective-permute-start.1
  6.3 0.0 copy-start
  6.4 4.0 %states.1 = (bf16[4,8,256,128]{3,2,1,0:T(8,128)(2,1)S(1)}, bf16[4,8,256,128]{3,2,1,0:T(8,128)(2,1)S(1)}, bf16[3,8,128,128]{3,2,1,0:T(8,128)(2,1)S(1)}, f32[8,128,128]{2,1,0:T(8,128)S(1)}) custom-call(bf16[1024,8,128]{2,1,0:T(8,128)(2,1)} %k_ref.1, bf16[1024,8,128]{2,1,0:T(8,128)(2,1)} %v_ref.1), custom_call_target="tpu_custom_call" | custom-call | flops 268435456 | bytes 8388608 | tf_op jit(solution)/shard_map/states/pallas_call | solution.py:357
  10.4 0.0 collective-permute-done
  10.4 0.0 collective-permute-done.2
  10.4 1.0 %collective-permute-done.1 = s32[21,256]{1,0:T(8,128)S(1)} collective-permute-done((s32[21,256]{1,0:T(8,128)}, s32[21,256]{1,0:T(8,128)S(1)}, u32[]{:S(2)}, u32[]{:S(2)}) %collective-permute-start.1) | collective-permute-done | bytes 21536 | tf_op jit(solution)/shard_map/ppermute | solution.py:376
  11.4 0.0 copy-done
  11.4 0.1 fusion.lam_ref
  11.5 4.8 %level_grads.1 = (bf16[4,8,256,128]{3,2,1,0:T(8,128)(2,1)S(1)}, bf16[4,8,128,256]{3,2,1,0:T(8,128)(2,1)S(1)}, f32[20,128,128]{2,1,0:T(8,128)S(1)}, f32[12,128,128]{2,1,0:T(8,128)S(1)}) custom-call(f32[14,1024]{1,0:T(8,128)S(1)} %fusion.lam_ref, bf16[1024,8,128]{2,1,0:T(8,128)(2,1)} %q_ref.1, bf16[1024,8,128]{2,1,0:T(8,128)(2,1)} %g_ref.1, ...), custom_call_target="tpu_custom_call" | custom-call | flops 805306368 | bytes 8388608 | tf_op jit(solution)/shard_map/level_grads/pallas_call | solution.py:394
  16.3 0.1 collective-permute-start.3
  16.4 2.1 %first_tile.1 = (f32[8,128,256]{2,1,0:T(8,128)S(1)}, bf16[4,8,256,128]{3,2,1,0:T(8,128)(2,1)S(1)}, bf16[4,8,256,128]{3,2,1,0:T(8,128)(2,1)S(1)}, bf16[4,8,256,128]{3,2,1,0:T(8,128)(2,1)S(1)}) custom-call(f32[14,1024]{1,0:T(8,128)S(1)} %fusion.lam_ref, bf16[4,8,256,128]{3,2,1,0:T(8,128)(2,1)S(1)} %get-tuple-element.49.k_ref, ...), custom_call_target="tpu_custom_call" | custom-call | flops 939524096 | bytes 4194304 | tf_op jit(solution)/shard_map/first_tile/pallas_call | solution.py:418
  18.4 0.9 %collective-permute-done.3.found_ref = f32[20,128,128]{2,1,0:T(8,128)S(1)} collective-permute-done((f32[20,128,128]{2,1,0:T(8,128)S(1)}, f32[20,128,128]{2,1,0:T(8,128)S(1)}, u32[]{:S(2)}, u32[]{:S(2)}) %collective-permute-start.3) | collective-permute-done | bytes 1310752 | tf_op jit(solution)/shard_map/ppermute | solution.py:332
  19.4 0.1 pair.1
  19.5 2.5 %collective-permute-start.4 = (f32[4,128,128]{2,1,0:T(8,128)S(1)}, f32[4,128,128]{2,1,0:T(8,128)S(1)}, u32[]{:S(2)}, u32[]{:S(2)}) collective-permute-start(f32[4,128,128]{2,1,0:T(8,128)S(1)} %get-tuple-element.62), channel_id=1, source_target_pairs={{0,24},{4,28},{8,16},{12,20},{16,8},{20,12},{24,0},{28,4},{1,25},{... | collective-permute-start | bytes 786440 | tf_op jit(solution)/shard_map/ppermute | solution.py:332
  22.0 0.5 %collective-permute-start.5 = (f32[4,128,128]{2,1,0:T(8,128)S(1)}, f32[4,128,128]{2,1,0:T(8,128)S(1)}, u32[]{:S(2)}, u32[]{:S(2)}) collective-permute-start(f32[4,128,128]{2,1,0:T(8,128)S(1)} %get-tuple-element.63), channel_id=1, source_target_pairs={{0,8},{4,12},{8,0},{12,4},{16,24},{20,28},{24,16},{28,20},{1,9},{5... | collective-permute-start | bytes 786440 | tf_op jit(solution)/shard_map/ppermute | solution.py:332
  22.5 0.5 %collective-permute-start.6 = (f32[4,128,128]{2,1,0:T(8,128)S(1)}, f32[4,128,128]{2,1,0:T(8,128)S(1)}, u32[]{:S(2)}, u32[]{:S(2)}) collective-permute-start(f32[4,128,128]{2,1,0:T(8,128)S(1)} %get-tuple-element.64), channel_id=1, source_target_pairs={{0,16},{4,20},{8,24},{12,28},{16,0},{20,4},{24,8},{28,12},{1,17},{... | collective-permute-start | bytes 786440 | tf_op jit(solution)/shard_map/ppermute | solution.py:332
  23.0 9.0 %local.1 = (bf16[4,8,256,128]{3,2,1,0:T(8,128)(2,1)S(1)}, bf16[4,8,256,128]{3,2,1,0:T(8,128)(2,1)S(1)}, bf16[4,8,256,128]{3,2,1,0:T(8,128)(2,1)S(1)}, f32[4,8,128,128]{3,2,1,0:T(8,128)S(1)}) custom-call(f32[14,1024]{1,0:T(8,128)S(1)} %fusion.lam_ref, ...), custom_call_target="tpu_custom_call", output_to_operand_aliasing={{0}: (8, {}), {1}: (9, {}), {2}: (10, {})} | custom-call | flops 3758096384 | bytes 4194304 | tf_op jit(solution)/shard_map/local/pallas_call | solution.py:441
  32.1 0.0 collective-permute-done.4.refs_0_
  32.1 2.4 %collective-permute-done.5.refs_1_ = f32[4,128,128]{2,1,0:T(8,128)S(1)} collective-permute-done((f32[4,128,128]{2,1,0:T(8,128)S(1)}, f32[4,128,128]{2,1,0:T(8,128)S(1)}, u32[]{:S(2)}, u32[]{:S(2)}) %collective-permute-start.5) | collective-permute-done | bytes 262176 | tf_op jit(solution)/shard_map/ppermute | solution.py:332
  34.5 0.0 collective-permute-done.6.refs_2_
  34.6 0.1 collective-permute-start.7
  34.6 1.3 %own_half.1 = (bf16[4,8,256,128]{3,2,1,0:T(8,128)(2,1)S(1)}, bf16[4,8,256,128]{3,2,1,0:T(8,128)(2,1)S(1)}, bf16[4,8,256,128]{3,2,1,0:T(8,128)(2,1)S(1)}) custom-call(f32[14,1024]{1,0:T(8,128)S(1)} %fusion.lam_ref, bf16[4,8,256,128]{3,2,1,0:T(8,128)(2,1)S(1)} %get-tuple-element.49.k_ref, ...), custom_call_target="tpu_custom_call", output_to_operand_aliasing={{0}: (6, {}), {1}: (7, {}), {2}: (8, {})} | custom-call | flops 671088640 | bytes 8388608 | tf_op jit(solution)/shard_map/own_half/pallas_call | solution.py:471
  36.0 0.5 %collective-permute-done.7.sums_ref = f32[2,4,128,128]{3,2,1,0:T(8,128)S(1)} collective-permute-done((f32[2,4,128,128]{3,2,1,0:T(8,128)S(1)}, f32[2,4,128,128]{3,2,1,0:T(8,128)S(1)}, u32[]{:S(2)}, u32[]{:S(2)}) %collective-permute-start.7) | collective-permute-done | bytes 524320 | tf_op jit(solution)/shard_map/ppermute | solution.py:332
  36.5 4.7 %final.1 = (bf16[1024,8,128]{2,1,0:T(8,128)(2,1)}, bf16[1024,8,128]{2,1,0:T(8,128)(2,1)}, bf16[1024,8,128]{2,1,0:T(8,128)(2,1)}) custom-call(f32[14,1024]{1,0:T(8,128)S(1)} %fusion.lam_ref, bf16[4,8,256,128]{3,2,1,0:T(8,128)(2,1)S(1)} %get-tuple-element.49.k_ref, bf16[4,8,256,128]{3,2,1,0:T(8,128)(2,1)S(1)} %get-tuple-element.50.v_ref, ...), custom_call_target="tpu_custom_call" | custom-call | flops 671088640 | bytes 16777216 | tf_op jit(solution)/shard_map/final/pallas_call | solution.py:483
  (4 shorter events, 0.1 us)
Async XLA Ops:
  0.6 9.8 %collective-permute-start = (s32[21,256]{1,0:T(8,128)}, s32[21,256]{1,0:T(8,128)S(1)}, u32[]{:S(2)}, u32[]{:S(2)}) collective-permute-start(s32[21,256]{1,0:T(8,128)} %param.9), channel_id=1, source_target_pairs={{0,1},{1,0},{2,3},{3,2},{4,5},{5,4},{6,7},{7,6},{8,9},{9,8},{10,11... | collective-permute-start | bytes 64520 | tf_op jit(solution)/shard_map/ppermute | solution.py:376
  3.7 6.7 %collective-permute-start.2 = (s32[21,256]{1,0:T(8,128)}, s32[21,256]{1,0:T(8,128)S(1)}, u32[]{:S(2)}, u32[]{:S(2)}) collective-permute-start(s32[21,256]{1,0:T(8,128)} %param.9), channel_id=1, source_target_pairs={{0,3},{1,2},{2,1},{3,0},{4,7},{5,6},{6,5},{7,4},{8,11},{9,10},{10,... | collective-permute-start | bytes 64520 | tf_op jit(solution)/shard_map/ppermute | solution.py:376
  6.2 5.2 %collective-permute-start.1 = (s32[21,256]{1,0:T(8,128)}, s32[21,256]{1,0:T(8,128)S(1)}, u32[]{:S(2)}, u32[]{:S(2)}) collective-permute-start(s32[21,256]{1,0:T(8,128)} %param.9), channel_id=1, source_target_pairs={{0,2},{1,3},{2,0},{3,1},{4,6},{5,7},{6,4},{7,5},{8,10},{9,11},{10,... | collective-permute-start | bytes 64520 | tf_op jit(solution)/shard_map/ppermute | solution.py:376
  6.3 5.1 %copy-start = (s32[21,256]{1,0:T(8,128)S(1)}, s32[21,256]{1,0:T(8,128)}, u32[]{:S(2)}) copy-start(s32[21,256]{1,0:T(8,128)} %param.9) | copy-start | bytes 64516
  16.3 3.1 %collective-permute-start.3 = (f32[20,128,128]{2,1,0:T(8,128)S(1)}, f32[20,128,128]{2,1,0:T(8,128)S(1)}, u32[]{:S(2)}, u32[]{:S(2)}) collective-permute-start(f32[20,128,128]{2,1,0:T(8,128)S(1)} %get-tuple-element.54), channel_id=1, source_target_pairs={{0,4},{4,0},{8,12},{12,8},{16,20},{20,16},{24,28},{28,24},{1,5},{5... | collective-permute-start | bytes 3932168 | tf_op jit(solution)/shard_map/ppermute | solution.py:332
  19.5 12.6 %collective-permute-start.4 = (f32[4,128,128]{2,1,0:T(8,128)S(1)}, f32[4,128,128]{2,1,0:T(8,128)S(1)}, u32[]{:S(2)}, u32[]{:S(2)}) collective-permute-start(f32[4,128,128]{2,1,0:T(8,128)S(1)} %get-tuple-element.62), channel_id=1, source_target_pairs={{0,24},{4,28},{8,16},{12,20},{16,8},{20,12},{24,0},{28,4},{1,25},{... | collective-permute-start | bytes 786440 | tf_op jit(solution)/shard_map/ppermute | solution.py:332
  22.0 12.5 %collective-permute-start.5 = (f32[4,128,128]{2,1,0:T(8,128)S(1)}, f32[4,128,128]{2,1,0:T(8,128)S(1)}, u32[]{:S(2)}, u32[]{:S(2)}) collective-permute-start(f32[4,128,128]{2,1,0:T(8,128)S(1)} %get-tuple-element.63), channel_id=1, source_target_pairs={{0,8},{4,12},{8,0},{12,4},{16,24},{20,28},{24,16},{28,20},{1,9},{5... | collective-permute-start | bytes 786440 | tf_op jit(solution)/shard_map/ppermute | solution.py:332
  22.5 12.0 %collective-permute-start.6 = (f32[4,128,128]{2,1,0:T(8,128)S(1)}, f32[4,128,128]{2,1,0:T(8,128)S(1)}, u32[]{:S(2)}, u32[]{:S(2)}) collective-permute-start(f32[4,128,128]{2,1,0:T(8,128)S(1)} %get-tuple-element.64), channel_id=1, source_target_pairs={{0,16},{4,20},{8,24},{12,28},{16,0},{20,4},{24,8},{28,12},{1,17},{... | collective-permute-start | bytes 786440 | tf_op jit(solution)/shard_map/ppermute | solution.py:332
  34.6 2.0 %collective-permute-start.7 = (f32[2,4,128,128]{3,2,1,0:T(8,128)S(1)}, f32[2,4,128,128]{3,2,1,0:T(8,128)S(1)}, u32[]{:S(2)}, u32[]{:S(2)}) collective-permute-start(f32[2,4,128,128]{3,2,1,0:T(8,128)S(1)} %sums.1.sums_ref), channel_id=1, source_target_pairs={{0,4},{4,0},{8,12},{12,8},{16,20},{20,16},{24,28},{28,24},{1,5},{5... | collective-permute-start | bytes 1572872 | tf_op jit(solution)/shard_map/ppermute | solution.py:332
